TPU v7x, 256 devices: a whole 4x4x8 slice. The times are simulated.
256 devices in a mesh: panel: 64 (over y, x, z_lo), slab: 4 (over z_hi, core).
Axes of the slice: x: 4, y: 4, z: 8 (z_hi: 2, z_lo: 4; z = z_hi * 4 + z_lo), core: 2. Of those that a mesh axis runs over, the one named last changes fastest.
Arguments:
- clip_cache: float32 [1024, 8192], P(None, 'panel'), may hold values from -6 to 6
- dose_scale: float32 [16, 8192], P(None, 'panel'), may hold values from 0.3 to 3
- focus_term: float32 [8, 8192], P(None, 'panel'), may hold values from -3 to 3
- clip_ids: int32 [32768], P('slab'), may hold values from 0 to 1023
- dose_ids: int32 [32768], P('slab'), may hold values from 0 to 15
- focus_ids: int32 [32768], P('slab'), may hold values from 0 to 7
Outputs:
- rotated: float32 [32768, 8192], P('slab', 'panel')
All inputs are finite; a program needn't handle non-finite values.
Results may differ from a plain program's by a relative error of at most 0.0001.
Values sent between devices are 32-bit elements; how exact they have to be, the bound alone decides.
A program may use at most 64 MiB of HBM per device.

v0:
```python
import jax
import jax.numpy as jnp
from jax import lax
from jax.sharding import PartitionSpec as P

ROUNDS = 2


EPSILON = 1e-06


def from_behind(block, axis, distance):
    devices = range(lax.axis_size(axis))
    route = [((i - distance) % len(devices), i) for i in devices]
    return lax.ppermute(block, axis, route)


def from_partner(value, axis, distance):
    mask = 2**distance
    pairs = [(source, source ^ mask) for source in range(lax.axis_size(axis))]
    return lax.ppermute(value, axis, pairs)


def block_rotation(gram):
    doubled = gram.shape[0]
    half_size = doubled // 2
    diagonal = jnp.diagonal(gram)
    coupling = gram / (diagonal[:, None] + diagonal[None, :])
    positions = lax.iota(jnp.int32, doubled)
    upper_mask = (positions[:, None] < half_size) & (positions[None, :] >= half_size)
    lower_mask = (positions[:, None] >= half_size) & (positions[None, :] < half_size)
    generator = 0.5 * (jnp.where(upper_mask, coupling, 0.0) - jnp.where(lower_mask, coupling, 0.0))
    identity = jnp.eye(doubled, dtype=gram.dtype)
    plus_half = identity + generator
    symmetric = identity + jnp.dot(
        generator.T, generator, precision=lax.Precision.HIGHEST, preferred_element_type=jnp.float32
    )
    factor = jnp.linalg.cholesky(symmetric)
    numerator = jnp.dot(
        plus_half, plus_half, precision=lax.Precision.HIGHEST, preferred_element_type=jnp.float32
    )
    return jax.scipy.linalg.cho_solve((factor, True), numerator)


def lookup(table_rows, indices):
    positions = lax.iota(jnp.int32, table_rows.shape[0])
    one_hot = (positions[:, None] == indices[None, :]).astype(jnp.float32)
    return lax.dot_general(
        one_hot,
        table_rows,
        (((0,), (0,)), ((), ())),
        precision=lax.Precision.HIGHEST,
        preferred_element_type=jnp.float32,
    )


def slab_gram(pair_block):
    gram_local = lax.dot_general(
        pair_block,
        pair_block,
        (((0,), (0,)), ((), ())),
        precision=lax.Precision.HIGHEST,
        preferred_element_type=jnp.float32,
    )
    return lax.psum(gram_local, "slab")


def product(left_side, right_side):
    return jnp.dot(
        left_side, right_side, precision=lax.Precision.HIGHEST, preferred_element_type=jnp.float32
    )


def shards(clip_cache, dose_scale, focus_term, clip_ids, dose_ids, focus_ids):
    row_count = clip_ids.shape[0]
    total_rows = row_count * lax.axis_size("slab")
    panel_width = clip_cache.shape[1]
    dose_part = lookup(dose_scale, dose_ids)
    focus_part = lookup(focus_term, focus_ids)
    jacobian = jnp.take(clip_cache, clip_ids, axis=0) * dose_part + focus_part
    col_squares = lax.psum(jnp.sum(jacobian * jacobian, axis=0), "slab")
    jacobian = jacobian * (1.0 / jnp.sqrt(col_squares / total_rows + EPSILON))
    seat_index = lax.axis_index("panel")
    is_odd = seat_index % 2 == 1
    own_start = seat_index % 2 * panel_width
    current = jacobian
    for section in range(ROUNDS):
        if section > 0:
            current = from_behind(current, "panel", 1)
        partner = from_partner(current, "panel", 0)
        pair_block = jnp.where(
            is_odd,
            jnp.concatenate([partner, current], axis=1),
            jnp.concatenate([current, partner], axis=1),
        )
        rotation = block_rotation(slab_gram(pair_block))
        own_cols = lax.dynamic_slice_in_dim(rotation, own_start, panel_width, 1)
        current = product(pair_block, own_cols)
    return current


def solution(mesh):
    return jax.shard_map(
        shards,
        mesh=mesh,
        in_specs=(
            P(None, "panel"),
            P(None, "panel"),
            P(None, "panel"),
            P("slab"),
            P("slab"),
            P("slab"),
        ),
        out_specs=P("slab", "panel"),
        check_vma=False,
    )
```

profile of v0, /device:TPU:1, one launch (start us, length us, event | category | flops | bytes accessed | tf_op | source)
XLA Modules:
  0.0 656.2 jit_solution(8444615578186647330)
XLA Ops:
  8.2 28.0 %gather_fusion = f32[8192,128]{1,0:T(8,128)} fusion(f32[1024,128]{1,0:T(8,128)S(1)} %copy-done, s32[8192]{0:T(1024)S(1)} %fusion.42), kind=kCustom, calls=%fused_computation | custom fusion | bytes 8421376 | tf_op jit(solution)/shard_map/jit(_take)/gather | solution.py:80
  36.1 5.7 copy.15
  41.8 4.2 convolution_multiply_fusion
  46.0 4.2 multiply_reduce_fusion
  50.2 12.1 %psum.21 = f32[128]{0:T(128)S(1)} all-reduce(f32[128]{0:T(128)S(1)} %get-tuple-element.51), channel_id=1, replica_groups=mesh['panel'=64,'slab'=4] {'slab'}, use_global_device_ids=true, to_apply=%region_1.2 | all-reduce | flops 128 | bytes 1024 | tf_op jit(solution)/shard_map/psum | solution.py:81
  62.3 4.7 broadcast_multiply_fusion
  67.7 85.9 %collective-permute-done = f32[8192,128]{0,1:T(8,128)} collective-permute-done((f32[8192,128]{0,1:T(8,128)}, f32[8192,128]{0,1:T(8,128)}, u32[]{:S(2)}, u32[]{:S(2)}) %collective-permute-start) | collective-permute-done | bytes 4194336 | tf_op jit(solution)/shard_map/ppermute | solution.py:21
  153.5 15.8 %fusion.3 = f32[256,256]{0,1:T(8,128)} fusion(f32[8192,128]{0,1:T(8,128)} %broadcast_multiply_fusion, f32[8192,128]{0,1:T(8,128)} %collective-permute-done, pred[]{:T(512)S(6)} %eq.42), kind=kOutput, calls=%fused_computation.14 | convolution fusion | flops 6448742400 | bytes 8650753 | tf_op jit(solution)/shard_map/dot_general | solution.py:58
  169.6 62.4 %all-reduce.4.cloned.1.call-done = f32[256,256]{0,1:T(8,128)} async-done(((f32[256,256]{0,1:T(8,128)}), f32[256,256]{0,1:T(8,128)}) %all-reduce.4.cloned.1.call-update) | async-done | bytes 262160 | tf_op jit(solution)/shard_map/psum | solution.py:65
  232.0 2.7 gather_fusion.1
  234.7 1.6 convolution_add_fusion.2
  236.5 11.7 %cholesky.130 = f32[128,128]{1,0:T(8,128)S(1)} custom-call(f32[128,128]{1,0:T(8,128)S(1)} %cholesky.194), custom_call_target="Cholesky" | custom-call | tf_op jit(solution)/shard_map/jit(cholesky)/cholesky | solution.py:38
  248.3 9.8 %custom-call.19 = f32[1,128,128]{1,2,0:T(8,128)S(1)} custom-call(f32[1,128,128]{2,1,0:T(8,128)S(1)} %get-tuple-element.50), custom_call_target="InvertDiagBlocksLowerTriangular" | custom-call | tf_op jit(solution)/shard_map/jit(cholesky)/cholesky | solution.py:38
  258.6 11.7 %cholesky.147 = f32[128,128]{1,0:T(8,128)S(1)} custom-call(f32[128,128]{1,0:T(8,128)S(1)} %convolution_subtract_fusion.5), custom_call_target="Cholesky" | custom-call | tf_op jit(solution)/shard_map/jit(cholesky)/cholesky | solution.py:38
  273.1 4.2 while.4
  273.9 1.4 bitcast_dynamic-update-slice_fusion.4
  275.9 1.4 bitcast_dynamic-update-slice_fusion.4
  277.3 19.7 %custom-call.20 = f32[2,128,128]{1,2,0:T(8,128)S(1)} custom-call(f32[2,128,128]{2,1,0:T(8,128)S(1)} %get-tuple-element.21), custom_call_target="InvertDiagBlocksLowerTriangular" | custom-call | tf_op jit(solution)/shard_map/jit(_cho_solve)/triangular_solve | solution.py:42
  299.6 8.8 %fusion.2 = f32[8192,128]{0,1:T(8,128)S(1)} fusion(f32[8192,128]{0,1:T(8,128)} %broadcast_multiply_fusion, f32[8192,128]{0,1:T(8,128)} %collective-permute-done, pred[]{:T(512)S(6)} %eq.42, s32[]{:T(128)S(6)} %select_n.63, f32[128,256]{1,0:T(8,128)S(1)} %fusion.32, f32[128,256]{1,0:T(8,128)S(1)} %fusion.33), kind=kOutput, calls=%fused_computation.13 | convolution fusion | flops 3227549696 | bytes 12845061 | tf_op jit(solution)/shard_map/dot_general | solution.py:69
  308.4 98.5 %collective-permute-done.1 = f32[8192,128]{0,1:T(8,128)S(1)} collective-permute-done((f32[8192,128]{0,1:T(8,128)S(1)}, f32[8192,128]{0,1:T(8,128)S(1)}, u32[]{:S(2)}, u32[]{:S(2)}) %collective-permute-start.1) | collective-permute-done | bytes 4194336 | tf_op jit(solution)/shard_map/ppermute | solution.py:15
  406.9 1.9 copy-done.7
  408.8 91.7 %collective-permute-done.2 = f32[8192,128]{0,1:T(8,128)} collective-permute-done((f32[8192,128]{0,1:T(8,128)S(1)}, f32[8192,128]{0,1:T(8,128)}, u32[]{:S(2)}, u32[]{:S(2)}) %collective-permute-start.2) | collective-permute-done | bytes 4194336 | tf_op jit(solution)/shard_map/ppermute | solution.py:21
  500.5 15.4 %fusion.1 = f32[256,256]{0,1:T(8,128)} fusion(f32[8192,128]{0,1:T(8,128)} %copy-done.7, f32[8192,128]{0,1:T(8,128)} %collective-permute-done.2, pred[]{:T(512)S(6)} %eq.42), kind=kOutput, calls=%fused_computation.12 | convolution fusion | flops 6448742400 | bytes 8650753 | tf_op jit(solution)/shard_map/dot_general | solution.py:58
  516.0 47.7 %all-reduce.6.cloned.1.call-done = f32[256,256]{0,1:T(8,128)} async-done(((f32[256,256]{0,1:T(8,128)}), f32[256,256]{0,1:T(8,128)}) %all-reduce.6.cloned.1.call-update) | async-done | bytes 262160 | tf_op jit(solution)/shard_map/psum | solution.py:65
  563.7 2.7 gather_fusion.2
  566.4 1.6 convolution_add_fusion.1
  568.3 11.7 %cholesky.164 = f32[128,128]{1,0:T(8,128)S(1)} custom-call(f32[128,128]{1,0:T(8,128)S(1)} %cholesky.197), custom_call_target="Cholesky" | custom-call | tf_op jit(solution)/shard_map/jit(cholesky)/cholesky | solution.py:38
  580.0 9.8 %custom-call.21 = f32[1,128,128]{1,2,0:T(8,128)S(1)} custom-call(f32[1,128,128]{2,1,0:T(8,128)S(1)} %get-tuple-element.46), custom_call_target="InvertDiagBlocksLowerTriangular" | custom-call | tf_op jit(solution)/shard_map/jit(cholesky)/cholesky | solution.py:38
  590.3 11.7 %cholesky.181 = f32[128,128]{1,0:T(8,128)S(1)} custom-call(f32[128,128]{1,0:T(8,128)S(1)} %convolution_subtract_fusion.4), custom_call_target="Cholesky" | custom-call | tf_op jit(solution)/shard_map/jit(cholesky)/cholesky | solution.py:38
  604.6 3.8 while.5
  608.5 19.8 %custom-call.22 = f32[2,128,128]{1,2,0:T(8,128)S(1)} custom-call(f32[2,128,128]{2,1,0:T(8,128)S(1)} %get-tuple-element.22), custom_call_target="InvertDiagBlocksLowerTriangular" | custom-call | tf_op jit(solution)/shard_map/jit(_cho_solve)/triangular_solve | solution.py:42
  630.9 18.2 %fusion = f32[8192,128]{1,0:T(8,128)} fusion(f32[8192,128]{0,1:T(8,128)} %copy-done.7, f32[8192,128]{0,1:T(8,128)} %collective-permute-done.2, pred[]{:T(512)S(6)} %eq.42, s32[]{:T(128)S(6)} %select_n.63, f32[128,256]{1,0:T(8,128)S(1)} %fusion.35, f32[128,256]{1,0:T(8,128)S(1)} %fusion.36), kind=kOutput, calls=%fused_computation.11 | convolution fusion | flops 3227549696 | bytes 12845061 | tf_op jit(solution)/shard_map/dot_general | solution.py:69
  (77 shorter events, 17.0 us)
Async XLA Ops:
  6.5 1.6 copy-start
  6.5 225.5 %all-reduce.4.cloned.1.call-start = ((), (), s32[]{:S(2)}) async-start(), calls=%async_computation | async-start | bytes 524288 | tf_op jit(solution)/shard_map/psum | solution.py:65
  36.1 5.7 copy-start.3
  36.1 5.7 copy-start.5
  41.8 4.2 copy-start.4
  41.8 4.2 copy-start.6
  67.0 86.5 %collective-permute-start = (f32[8192,128]{0,1:T(8,128)}, f32[8192,128]{0,1:T(8,128)}, u32[]{:S(2)}, u32[]{:S(2)}) collective-permute-start(f32[8192,128]{0,1:T(8,128)} %broadcast_multiply_fusion), channel_id=1, source_target_pairs={{0,4},{4,0},{8,12},{12,8},{16,20},{20,16},{24,28},{28,24},{32,36},... | collective-permute-start | bytes 12582920 | tf_op jit(solution)/shard_map/ppermute | solution.py:21
  169.4 394.4 %all-reduce.6.cloned.1.call-start = ((), (), s32[]{:S(2)}) async-start(), calls=%async_computation.1 | async-start | bytes 524288 | tf_op jit(solution)/shard_map/psum | solution.py:65
  232.0 65.0 %copy-start.1 = (f32[256,256]{0,1:T(8,128)S(1)}, f32[256,256]{0,1:T(8,128)}, u32[]{:S(2)}) copy-start(f32[256,256]{0,1:T(8,128)} %all-reduce.4.cloned.1.call-done) | copy-start | bytes 786436
  308.3 98.6 %collective-permute-start.1 = (f32[8192,128]{0,1:T(8,128)S(1)}, f32[8192,128]{0,1:T(8,128)S(1)}, u32[]{:S(2)}, u32[]{:S(2)}) collective-permute-start(f32[8192,128]{0,1:T(8,128)S(1)} %fusion.2), channel_id=1, source_target_pairs={{252,0},{0,4},{4,8},{8,12},{12,16},{16,20},{20,24},{24,28},{28,32}... | collective-permute-start | bytes 12582920 | tf_op jit(solution)/shard_map/ppermute | solution.py:15
  406.9 1.9 copy-start.7
  408.8 91.7 %collective-permute-start.2 = (f32[8192,128]{0,1:T(8,128)S(1)}, f32[8192,128]{0,1:T(8,128)}, u32[]{:S(2)}, u32[]{:S(2)}) collective-permute-start(f32[8192,128]{0,1:T(8,128)S(1)} %collective-permute-done.1), channel_id=1, source_target_pairs={{0,4},{4,0},{8,12},{12,8},{16,20},{20,16},{24,28},{28,24},{32,36},... | collective-permute-start | bytes 12582920 | tf_op jit(solution)/shard_map/ppermute | solution.py:21
  563.7 64.6 %copy-start.2 = (f32[256,256]{0,1:T(8,128)S(1)}, f32[256,256]{0,1:T(8,128)}, u32[]{:S(2)}) copy-start(f32[256,256]{0,1:T(8,128)} %all-reduce.6.cloned.1.call-done) | copy-start | bytes 786436
Sparse Core Ops, SparseCore 0:
  169.5 62.4 all-reduce.3
  516.1 47.5 all-reduce.5
where the time goes:
time: 663 us; the launch traced here: 656 us
  waiting for transfers between devices  386 us (58%)
  other arithmetic  115 us (17%)
  matrix products  75.9 us (11%)
  local copies, waits for them, and re-layouts  49 us (7%)
  between operations  16.5 us (2%)
  blocking collectives  12.1 us (2%)
    ppermute x2, waiting for transfers between devices, from_partner(): return lax.ppermute(value, axis, pairs)  178 us
    psum x2, waiting for transfers between devices, slab_gram(): return lax.psum(gram_local, 'slab')  110 us
    ppermute x1, waiting for transfers between devices, from_behind(): return lax.ppermute(block, axis, route)  98.5 us
    another operation x14, other arithmetic, block_rotation(): factor = jnp.linalg.cholesky(symmetric)  69.2 us
    another operation x5, other arithmetic, block_rotation(): return jax.scipy.linalg.cho_solve((factor, True), numerator)  39.6 us
    gather x2, local copies, waits for them, and re-layouts, shards(): jacobian = jnp.take(clip_cache, clip_ids, axis=0) * dose_part + focus_part  33.6 us
    dot_general x2, matrix products, slab_gram(): lax.dot_general(pair_block, pair_block, (((0,), (0,)), ((), ())), precisi...  31.2 us
    dot_general x2, matrix products, product(): jnp.dot(left_side, right_side, precision=lax.Precision.HIGHEST, preferred...  27 us
  transfers between devices with their start and end apart: 5, of which 5 were waited for; matrix products, arithmetic and copies ran while one was open for 0% of the time, Pallas kernels for 0%

commit v1 on v0

v1 whole, which is shorter than its diff:
```python
import functools

import jax
import jax.numpy as jnp
from jax import lax
from jax.experimental import pallas as pl
from jax.experimental.pallas import tpu as pltpu
from jax.sharding import PartitionSpec as P

MESH = pl.DeviceIdType.MESH
EPSILON = 1e-06
F32 = jnp.float32
BF16 = jnp.bfloat16
ANY = pl.BlockSpec(memory_space=pl.ANY)
VMEM = pl.BlockSpec(memory_space=pltpu.VMEM)
SMEM = pl.BlockSpec(memory_space=pltpu.SMEM)


def exchange(seats, c_ref, d_ref, f_ref, i_ref, j_ref, k_ref, cs, ds, fs, ci, di, fi, local_sem, send_sem, recv_sem):
    seat = lax.axis_index("panel")
    slab = lax.axis_index("slab")
    z_hi, core = slab // 2, slab % 2
    side = seat % 2
    base = seat - side
    nclip = c_ref.shape[0]
    half = nclip // 2

    def near(target):
        z_lo = target % 4
        other = jnp.where((z_lo == 0) | (z_lo == 3), 1, 0)
        return (z_hi + other) % 2

    partner = (seat + 1 - 2 * side, slab)
    next0 = (base + 2) % seats
    next1 = (base + 3) % seats
    to_next0 = (next0, near(next0) * 2 + core)
    to_next1 = (next1, near(next1) * 2 + core)
    from_group = near(seat) * 2 + core
    from_prev0 = ((base + seats - 2) % seats, from_group)
    from_prev1 = ((base + seats - 1) % seats, from_group)
    z_lo = seat % 4
    mirror = (seat - z_lo + 3 - z_lo, (1 - z_hi) * 2 + core)
    twin = (seat, z_hi * 2 + 1 - core)

    barrier = pltpu.get_barrier_semaphore()
    for device in (partner, from_prev0, from_prev1, mirror, twin):
        pl.semaphore_signal(barrier, inc=1, device_id=device, device_id_type=MESH)
    pl.semaphore_wait(barrier, 5)

    def remote(number, source, target, device, arrival=None):
        return pltpu.make_async_remote_copy(
            src_ref=source,
            dst_ref=target,
            send_sem=send_sem.at[number],
            recv_sem=recv_sem.at[number if arrival is None else arrival],
            device_id=device,
            device_id_type=MESH,
        )

    mine = pl.ds(pl.multiple_of(core * half, 8), half)
    own = 2 + side
    mate = 3 - side
    ids = (i_ref, ci), (j_ref, di), (k_ref, fi)

    sent = []
    for n, (source, target) in enumerate(ids):
        sent.append(remote(n, source, target.at[1], mirror))
    sent.append(remote(9, c_ref.at[mine], cs.at[own, mine], partner))
    sent.append(remote(12, d_ref, ds.at[own], partner))
    sent.append(remote(15, f_ref, fs.at[own], partner))
    for n, device in enumerate((to_next0, to_next1)):
        sent.append(remote(10 + n, c_ref.at[mine], cs.at[side, mine], device, 10 + side))
        sent.append(remote(13 + n, d_ref, ds.at[side], device, 13 + side))
        sent.append(remote(16 + n, f_ref, fs.at[side], device, 16 + side))
    for n, (source, target) in enumerate(ids):
        sent.append(remote(3 + n, source, target.at[2], twin))
    for copy in sent:
        copy.start()
    local = [
        pltpu.make_async_copy(c_ref, cs.at[own], local_sem.at[0]),
        pltpu.make_async_copy(d_ref, ds.at[own], local_sem.at[1]),
        pltpu.make_async_copy(f_ref, fs.at[own], local_sem.at[2]),
    ]
    for n, (source, target) in enumerate(ids):
        local.append(pltpu.make_async_copy(source, target.at[0], local_sem.at[3 + n]))
    for copy in local:
        copy.start()

    for n, (source, target) in enumerate(ids):
        remote(n, source, target.at[1], mirror).wait_recv()
        forward = remote(6 + n, target.at[1], target.at[3], twin)
        forward.start()
        sent.append(forward)
    for n, slot in ((9, mate), (10, 0), (11, 1)):
        remote(n, c_ref.at[mine], cs.at[slot, mine], partner).wait_recv()
        forward = remote(9 + n, cs.at[slot, mine], cs.at[slot, mine], twin)
        forward.start()
        sent.append(forward)
    for n, slot in ((12, mate), (13, 0), (14, 1)):
        remote(n, d_ref, ds.at[slot], partner).wait_recv()
        remote(n + 3, f_ref, fs.at[slot], partner).wait_recv()
    for n, (source, target) in enumerate(ids):
        remote(3 + n, source, target.at[2], twin).wait_recv()
        remote(6 + n, source, target.at[3], twin).wait_recv()
    theirs = pl.ds(pl.multiple_of((1 - core) * half, 8), half)
    for n, slot in ((18, mate), (19, 0), (20, 1)):
        remote(n, c_ref.at[theirs], cs.at[slot, theirs], twin).wait_recv()
    for copy in sent:
        copy.wait_send()
    for copy in local:
        copy.wait()


def gather_tables(seats, clip_cache, dose_scale, focus_term, ids):
    rows, cols = ids[0].shape
    out = [
        jax.ShapeDtypeStruct((4, *clip_cache.shape), F32),
        jax.ShapeDtypeStruct((4, *dose_scale.shape), F32),
        jax.ShapeDtypeStruct((4, *focus_term.shape), F32),
    ] + [jax.ShapeDtypeStruct((4, rows, cols), jnp.int32)] * 3
    return pl.pallas_call(
        functools.partial(exchange, seats),
        out_shape=out,
        in_specs=[ANY] * 6,
        out_specs=[ANY] * 6,
        scratch_shapes=[
            pltpu.SemaphoreType.DMA((6,)),
            pltpu.SemaphoreType.DMA((21,)),
            pltpu.SemaphoreType.DMA((21,)),
        ],
        compiler_params=pltpu.CompilerParams(collective_id=0, has_side_effects=True),
        name="exchange",
    )(clip_cache, dose_scale, focus_term, *ids)


def split(value):
    high = value.astype(BF16)
    return high, (value - high.astype(F32)).astype(BF16)


def dot(a, b, dims=((1,), (0,))):
    return lax.dot_general(a, b, (dims, ((), ())), preferred_element_type=F32)


def three(value):
    high = value.astype(BF16)
    rest = value - high.astype(F32)
    middle = rest.astype(BF16)
    return high, middle, (rest - middle.astype(F32)).astype(BF16)


def full(a, b, dims=((1,), (0,))):
    a1, a2, a3 = three(a)
    b1, b2, b3 = three(b)
    small = dot(a2, b2, dims) + dot(a1, b3, dims) + dot(a3, b1, dims)
    return dot(a1, b1, dims) + (dot(a1, b2, dims) + dot(a2, b1, dims) + small)


TN = ((0,), (0,))
NT = ((1,), (1,))


def column(row):
    return jnp.broadcast_to(row, (128, row.shape[1])).T[:, :1]


def inverses(bs, state):
    n = bs[0].shape[0]
    eye = (lax.broadcasted_iota(jnp.int32, (n, n), 0) == lax.broadcasted_iota(jnp.int32, (n, n), 1)).astype(F32)
    squares = [full(b, b, NT) for b in bs]
    bound = functools.reduce(jnp.maximum, [jnp.max(jnp.sum(jnp.abs(s), axis=1)) for s in squares])
    scale = 2.0 / (2.0 + bound)
    for e, s in enumerate(squares):
        rest = (1.0 - scale) * eye - scale * s
        state[e, :n, :] = scale * (eye + rest)
        state[e, n:, :] = full(rest, rest)
    ratio = bound / (2.0 + bound)

    def body(ratio):
        for e in range(len(bs)):
            old = state[e]
            new = full(old, old[n:])
            state[e, :n, :] = old[:n] + new[:n]
            state[e, n:, :] = new[n:]
        return ratio * ratio

    lax.while_loop(lambda ratio: ratio > 1e-8, body, ratio * ratio)
    return [state[e, :n, :] for e in range(len(bs))], eye


def compute(
    total, cs, ds, fs, ci, di, fi, clip_ids, dose_ids, focus_ids, out,
    ch, cl, ct, counts, drow, dcol, gram, table, fw, wd, state,
):
    nclip, width = cs.shape[1:]
    ndose, nfocus = ds.shape[1], fs.shape[1]
    cols = 4 * width
    for p in range(4):
        high, low = split(cs[p])
        lanes = pl.ds(p * width, width)
        ch[:, lanes] = high
        cl[:, lanes] = low
        ct[lanes, :] = cs[p].T
        drow[:, lanes] = ds[p]
        dcol[lanes, :] = jnp.concatenate([ds[p], jnp.zeros((128 - ndose, width), F32)], axis=0).T

    counts[...] = jnp.zeros_like(counts)
    tall = lax.broadcasted_iota(jnp.int32, (512, 128), 0)
    wide = lax.broadcasted_iota(jnp.int32, (256, 128), 0)
    step_rows = 8

    def count(step, _):
        slab = step // (ci.shape[1] // step_rows)
        rows = pl.ds(pl.multiple_of(step % (ci.shape[1] // step_rows) * step_rows, step_rows), step_rows)
        clip = ci[slab, rows, :]
        first = (clip // 256) * 128 + di[slab, rows, :] * nfocus + fi[slab, rows, :]
        second = clip % 256
        a = jnp.concatenate([(tall == first[r : r + 1, :]).astype(F32).astype(BF16) for r in range(step_rows)], axis=1)
        b = jnp.concatenate([(wide == second[r : r + 1, :]).astype(F32).astype(BF16) for r in range(step_rows)], axis=1)
        counts[...] += dot(a, b, NT)
        return 0

    lax.fori_loop(0, 4 * ci.shape[1] // step_rows, count, 0)

    n = jnp.concatenate([counts[h * 128 : (h + 1) * 128, :] for h in range(4)], axis=1)
    fall = jnp.concatenate([fs[p] for p in range(4)], axis=1)
    nh, nl = split(n)
    v = dot(nh, ch[...]) + dot(nh, cl[...]) + dot(nl, ch[...])
    s = jnp.zeros((nfocus, cols), F32)
    per_focus = jnp.zeros((nfocus, nclip), F32)
    for j in range(ndose):
        s = s + v[j * nfocus : (j + 1) * nfocus, :] * drow[j : j + 1, :]
        per_focus = per_focus + n[j * nfocus : (j + 1) * nfocus, :]
    nk = jnp.sum(per_focus, axis=1, keepdims=True)
    s = s + 0.5 * nk * fall
    gram[...] = full(jnp.concatenate([s, fall], axis=0), jnp.concatenate([fall, s], axis=0), TN)

    lane = lax.broadcasted_iota(jnp.int32, (cols, 128), 1)

    def dose(j, _):
        begin = pl.multiple_of(j * nfocus, nfocus)
        nj = jnp.concatenate(
            [jnp.sum(counts[pl.ds(h * 128 + begin, nfocus), :], axis=0, keepdims=True) for h in range(4)], axis=1
        )
        dj = jnp.sum(jnp.where(lane == j, dcol[...], 0.0), axis=1, keepdims=True)
        row = drow[pl.ds(j, 1), :]
        for m in range(2):
            here = pl.ds(m * 256, 256)
            right = pl.ds(m * 256, cols - m * 256)
            uh, ul = split(ct[here, :] * nj * dj[m * 256 : (m + 1) * 256, :])
            part = dot(uh, ch[:, right]) + dot(uh, cl[:, right]) + dot(ul, ch[:, right])
            gram[here, right] += part * row[:, m * 256 :]
        return 0

    lax.fori_loop(0, ndose, dose, 0)

    row_i = lax.broadcasted_iota(jnp.int32, (128, 128), 0)
    col_i = lax.broadcasted_iota(jnp.int32, (128, 128), 1)
    squares = jnp.concatenate(
        [
            jnp.sum(jnp.where(row_i == col_i, gram[p * 128 : (p + 1) * 128, p * 128 : (p + 1) * 128], 0.0), axis=0, keepdims=True)
            for p in range(4)
        ],
        axis=1,
    )
    inverse_norm = 1.0 / jnp.sqrt(squares / total + EPSILON)
    norm_col = column(inverse_norm)
    d = squares * inverse_norm * inverse_norm
    d_col = column(d)
    g_prev = gram[:256, :256] * norm_col[:256] * inverse_norm[:, :256]
    g_cross = gram[:256, 256:] * norm_col[:256] * inverse_norm[:, 256:]
    g_own = gram[256:, 256:] * norm_col[256:] * inverse_norm[:, 256:]
    b_prev = 0.5 * g_prev[:128, 128:] / (d_col[:128] + d[:, 128:256])
    b_own = 0.5 * g_own[:128, 128:] / (d_col[256:384] + d[:, 384:])
    (m_prev, m_own), eye = inverses([b_prev, b_own], state)
    z = 2.0 * full(m_prev, b_prev)
    q_right = jnp.concatenate([z, eye - full(b_prev, z, TN)], axis=0)
    q_left = jnp.concatenate([2.0 * m_own - eye, -2.0 * full(b_own, m_own, TN)], axis=0)

    cross = full(full(q_right, g_cross, TN), q_left)
    d_left = jnp.sum(q_right * full(g_prev, q_right), axis=0, keepdims=True)
    d_right = jnp.sum(q_left * full(g_own, q_left), axis=0, keepdims=True)
    b = 0.5 * cross / (column(d_left) + d_right)
    (m,), _ = inverses([b], state)
    z = 2.0 * full(m, b)
    odd = lax.axis_index("panel") % 2 == 1
    top = jnp.where(odd, z, 2.0 * m - eye)
    bottom = jnp.where(odd, eye - full(b, z, TN), -2.0 * full(b, m, TN))
    w = jnp.concatenate([full(q_right, top), full(q_left, bottom)], axis=0) * norm_col
    fw[...] = full(fall, w)

    wd[...] = w

    def rows_of(pair, _):
        parts = []
        for e in range(2):
            dj = jnp.sum(jnp.where(lane == pair * 2 + e, dcol[...], 0.0), axis=1, keepdims=True)
            parts.append(wd[...] * dj)
        wh, wl = split(jnp.concatenate(parts, axis=1))
        for m in range(nclip // 256):
            here = pl.ds(m * 256, 256)
            part = dot(ch[here, :], wh) + dot(cl[here, :], wh) + dot(ch[here, :], wl)
            for e in range(2):
                begin = pl.multiple_of((pair * 2 + e) * nclip + m * 256, 256)
                table[pl.ds(begin, 256), :] = part[:, e * 128 : (e + 1) * 128]
        return 0

    lax.fori_loop(0, ndose // 2, rows_of, 0)

    unroll = 16

    def gather(step, _):
        begin = pl.multiple_of(step * unroll, unroll)
        for u in range(unroll):
            r = begin + u
            where = dose_ids[r] * nclip + clip_ids[r]
            out[pl.ds(r, 1), :] = table[pl.ds(where, 1), :] + fw[pl.ds(focus_ids[r], 1), :]
        return 0

    lax.fori_loop(0, out.shape[0] // unroll, gather, 0)


def shards(clip_cache, dose_scale, focus_term, clip_ids, dose_ids, focus_ids):
    seats = lax.axis_size("panel")
    rows = clip_ids.shape[0]
    nclip, width = clip_cache.shape
    ndose = dose_scale.shape[0]
    ids = [a.reshape(rows // 128, 128) for a in (clip_ids, dose_ids, focus_ids)]
    gathered = gather_tables(seats, clip_cache, dose_scale, focus_term, ids)
    cols = 4 * width
    return pl.pallas_call(
        functools.partial(compute, float(rows * lax.axis_size("slab"))),
        out_shape=jax.ShapeDtypeStruct((rows, width), F32),
        in_specs=[VMEM] * 6 + [SMEM] * 3,
        out_specs=VMEM,
        scratch_shapes=[
            pltpu.VMEM((nclip, cols), BF16),
            pltpu.VMEM((nclip, cols), BF16),
            pltpu.VMEM((cols, nclip), F32),
            pltpu.VMEM((512, 256), F32),
            pltpu.VMEM((ndose, cols), F32),
            pltpu.VMEM((cols, 128), F32),
            pltpu.VMEM((cols, cols), F32),
            pltpu.VMEM((ndose * nclip, width), F32),
            pltpu.VMEM((focus_term.shape[0], width), F32),
            pltpu.VMEM((cols, width), F32),
            pltpu.VMEM((2, 2 * width, width), F32),
        ],
        compiler_params=pltpu.CompilerParams(vmem_limit_bytes=48 * 2**20),
        name="compute",
    )(*gathered, clip_ids, dose_ids, focus_ids)


def solution(mesh):
    return jax.shard_map(
        shards,
        mesh=mesh,
        in_specs=(
            P(None, "panel"),
            P(None, "panel"),
            P(None, "panel"),
            P("slab"),
            P("slab"),
            P("slab"),
        ),
        out_specs=P("slab", "panel"),
        check_vma=False,
    )
```

time: 663 us -> 123 us (0.19)
  waiting for transfers between devices: 386 us -> 0 us
  other arithmetic: 115 us -> 0 us
  Pallas kernels: 0 us -> 114 us
  matrix products: 75.9 us -> 0 us
  local copies, waits for them, and re-layouts: 49 us -> 8.04 us
  between operations: 16.5 us -> 0.03 us
  blocking collectives: 12.1 us -> 0 us
    ppermute x3 -> x0, waiting for transfers between devices: 276 us -> none  [the longest x2 178 us: from_partner(): return lax.ppermute(value, axis, pairs)]
    pallas_call x0 -> x2, Pallas kernels: none -> 114 us  [the longest x1 82.9 us: shards(): pl.pallas_call(functools.partial(compute, float(rows * lax.axis_size('sla...]
    psum x2 -> x0, waiting for transfers between devices: 110 us -> none  [slab_gram(): return lax.psum(gram_local, 'slab')]
    another operation x19 -> x0, other arithmetic: 109 us -> none  [the longest x14 69.2 us: block_rotation(): factor = jnp.linalg.cholesky(symmetric)]
    dot_general x10 -> x0, matrix products: 71.5 us -> none  [the longest x2 31.2 us: slab_gram(): lax.dot_general(pair_block, pair_block, (((0,), (0,)), ((), ())), precisi...]
    gather x4 -> x0, local copies, waits for them, and re-layouts: 38.9 us -> none  [the longest x2 33.6 us: shards(): jacobian = jnp.take(clip_cache, clip_ids, axis=0) * dose_part + focus_part]
    psum x1 -> x0, blocking collectives: 12.1 us -> none  [shards(): col_squares = lax.psum(jnp.sum(jacobian * jacobian, axis=0), 'slab')]
    another operation x19 -> x0, local copies, waits for them, and re-layouts: 7.84 us -> none  [the longest x15 7.79 us: block_rotation(): return jax.scipy.linalg.cho_solve((factor, True), numerator)]
  transfers between devices with their start and end apart: 5 -> 0, of which waited for: 5 -> 0; matrix products, arithmetic and copies ran while one was open for 0% -> 0% of each run, Pallas kernels for 0% -> 0%
where the time goes in v1:
time: 123 us; the launch traced here: 122 us
  Pallas kernels  114 us (93%)
  local copies, waits for them, and re-layouts  8.04 us (7%)
    pallas_call x1, Pallas kernels, shards(): pl.pallas_call(functools.partial(compute, float(rows * lax.axis_size('sla...  82.9 us
    pallas_call x1, Pallas kernels, gather_tables(): pl.pallas_call(functools.partial(exchange, seats), out_shape=out, in_spec...  31.4 us
    unnamed x18, local copies, waits for them, and re-layouts  8.04 us

profile of v1, /device:TPU:1, one launch (start us, length us, event | category | flops | bytes accessed | tf_op | source)
XLA Modules:
  0.0 122.4 jit_solution(16012314969938968776)
XLA Ops:
  0.0 31.4 %exchange.1 = (f32[4,1024,128]{2,1,0:T(8,128)}, f32[4,16,128]{2,1,0:T(8,128)}, f32[4,8,128]{2,1,0:T(8,128)}, s32[4,64,128]{2,1,0:T(8,128)}, s32[4,64,128]{2,1,0:T(8,128)}, /*index=5*/s32[4,64,128]{2,1,0:T(8,128)}) custom-call(f32[1024,128]{1,0:T(8,128)} %c_ref.1, f32[16,128]{1,0:T(8,128)} %d_ref.1, f32[8,128]{1,0:T(8,128)} %f_ref.1, s32[64,128]{1,0:T(8,128)} %bitcast.3, ...), custom_call_target="tpu_custom_call" | custom-call | tf_op jit(solution)/shard_map/exchange/pallas_call | solution.py:121
  31.4 0.0 copy-start
  31.4 1.6 %copy-done = f32[4,1024,128]{2,1,0:T(8,128)S(1)} copy-done((f32[4,1024,128]{2,1,0:T(8,128)S(1)}, f32[4,1024,128]{2,1,0:T(8,128)}, u32[]{:S(2)}) %copy-start) | copy-done | bytes 2097176
  33.0 0.0 copy-start.1
  33.0 0.9 copy-done.1
  33.9 0.0 copy-start.2
  33.9 0.9 copy-done.2
  34.8 0.0 copy-start.3
  34.8 0.9 copy-done.3
  35.7 0.0 copy-start.4
  35.7 0.8 copy-done.4
  36.5 0.0 copy-start.5
  36.5 0.8 copy-done.5
  37.3 0.0 copy-start.6
  37.3 0.8 copy-done.6
  38.0 0.0 copy-start.7
  38.0 0.8 copy-done.7
  38.8 0.0 copy-start.8
  38.8 0.7 copy-done.8
  39.5 82.9 %compute.1 = f32[8192,128]{1,0:T(8,128)} custom-call(f32[4,1024,128]{2,1,0:T(8,128)S(1)} %copy-done, f32[4,16,128]{2,1,0:T(8,128)S(1)} %copy-done.7, f32[4,8,128]{2,1,0:T(8,128)S(1)} %copy-done.8, s32[4,64,128]{2,1,0:T(8,128)S(1)} %copy-done.1, s32[4,64,128]{2,1,0:T(8,128)S(1)} %copy-done.2, s32[4,64,128]{2,1,0:T(8,128)S(1)} %copy-done.3, ...), custom_call_target="tpu_custom_call" | custom-call | tf_op jit(solution)/shard_map/compute/pallas_call | solution.py:331
Async XLA Ops:
  31.4 1.6 %copy-start = (f32[4,1024,128]{2,1,0:T(8,128)S(1)}, f32[4,1024,128]{2,1,0:T(8,128)}, u32[]{:S(2)}) copy-start(f32[4,1024,128]{2,1,0:T(8,128)} %get-tuple-element.11.cs) | copy-start | bytes 6291460
  33.0 0.9 copy-start.1
  33.9 0.9 copy-start.2
  34.8 0.9 copy-start.3
  35.7 0.8 copy-start.4
  36.5 0.8 copy-start.5
  37.3 0.8 copy-start.6
  38.0 0.8 copy-start.7
  38.8 0.7 copy-start.8

commit v2 on v1

v2 whole, which is shorter than its diff:
```python
import functools

import jax
import jax.numpy as jnp
from jax import lax
from jax.experimental import pallas as pl
from jax.experimental.pallas import tpu as pltpu
from jax.sharding import PartitionSpec as P

MESH = pl.DeviceIdType.MESH
EPSILON = 1e-06
F32 = jnp.float32
BF16 = jnp.bfloat16
ANY = pl.BlockSpec(memory_space=pl.ANY)
VMEM = pl.BlockSpec(memory_space=pltpu.VMEM)


def split(value):
    high = value.astype(BF16)
    return high, (value - high.astype(F32)).astype(BF16)


def dot(a, b, dims=((1,), (0,))):
    return lax.dot_general(a, b, (dims, ((), ())), preferred_element_type=F32)


def three(value):
    high = value.astype(BF16)
    rest = value - high.astype(F32)
    middle = rest.astype(BF16)
    return high, middle, (rest - middle.astype(F32)).astype(BF16)


def full(a, b, dims=((1,), (0,))):
    a1, a2, a3 = three(a)
    b1, b2, b3 = three(b)
    small = dot(a2, b2, dims) + dot(a1, b3, dims) + dot(a3, b1, dims)
    return dot(a1, b1, dims) + (dot(a1, b2, dims) + dot(a2, b1, dims) + small)


TN = ((0,), (0,))
NT = ((1,), (1,))


def column(row):
    return jnp.broadcast_to(row, (128, row.shape[1])).T[:, :1]


def inverses(bs, state):
    n = bs[0].shape[0]
    eye = (lax.broadcasted_iota(jnp.int32, (n, n), 0) == lax.broadcasted_iota(jnp.int32, (n, n), 1)).astype(F32)
    squares = [full(b, b, NT) for b in bs]
    bound = functools.reduce(jnp.maximum, [jnp.max(jnp.sum(jnp.abs(s), axis=1)) for s in squares])
    scale = 2.0 / (2.0 + bound)
    for e, s in enumerate(squares):
        rest = (1.0 - scale) * eye - scale * s
        state[e, :n, :] = scale * (eye + rest)
        state[e, n:, :] = full(rest, rest)
    ratio = bound / (2.0 + bound)

    def body(ratio):
        for e in range(len(bs)):
            old = state[e]
            new = full(old, old[n:])
            state[e, :n, :] = old[:n] + new[:n]
            state[e, n:, :] = new[n:]
        return ratio * ratio

    lax.while_loop(lambda ratio: ratio > 1e-8, body, ratio * ratio)
    return [state[e, :n, :] for e in range(len(bs))], eye


def onehot(places, count, offset):
    value = jnp.broadcast_to(places.astype(F32) - offset, (16, places.shape[1])).astype(BF16)
    tile = lax.broadcasted_iota(jnp.int32, (16, places.shape[1]), 0).astype(F32)
    one, none = jnp.ones_like(value), jnp.zeros_like(value)
    return [jnp.where((tile + 16.0 * t).astype(BF16) == value, one, none) for t in range(count // 16)]


def count_ids(counts, clips, doses, focuses):
    rows = 8

    def count(step, _):
        here = pl.ds(pl.multiple_of(step * rows, rows), rows)
        clip = clips[here, :]
        first = (clip // 256) * 128 + doses[here, :] * 8 + focuses[here, :]
        second = clip % 256
        tall, wide = [], []
        for r in range(rows):
            row = first[r : r + 1, :]
            tall.append(jnp.concatenate(onehot(row, 256, 0.0) + onehot(row, 256, 256.0), axis=0))
            wide.append(jnp.concatenate(onehot(second[r : r + 1, :], 256, 0.0), axis=0))
        counts[...] += dot(jnp.concatenate(tall, axis=1), jnp.concatenate(wide, axis=1), NT)
        return 0

    lax.fori_loop(0, clips.shape[0] // rows, count, 0)


def exchange(
    seats, c_ref, d_ref, f_ref, i_ref, j_ref, k_ref, ch_out, cl_out, ds_out, fs_out, gram_out,
    cs, ds, fs, ci, di, fi, counts, counts_twin, ch, cl, ct, drow, dcol, gram, gram_twin, send_sem, recv_sem, out_sem,
):
    seat = lax.axis_index("panel")
    slab = lax.axis_index("slab")
    z_hi, core = slab // 2, slab % 2
    side = seat % 2
    base = seat - side
    nclip, width = c_ref.shape
    ndose, nfocus = d_ref.shape[0], f_ref.shape[0]
    cols = 4 * width
    half = nclip // 2

    def near(target):
        z_lo = target % 4
        other = jnp.where((z_lo == 0) | (z_lo == 3), 1, 0)
        return (z_hi + other) % 2

    partner = (seat + 1 - 2 * side, slab)
    next0 = (base + 2) % seats
    next1 = (base + 3) % seats
    to_next0 = (next0, near(next0) * 2 + core)
    to_next1 = (next1, near(next1) * 2 + core)
    from_group = near(seat) * 2 + core
    from_prev0 = ((base + seats - 2) % seats, from_group)
    from_prev1 = ((base + seats - 1) % seats, from_group)
    z_lo = seat % 4
    mirror = (seat - z_lo + 3 - z_lo, (1 - z_hi) * 2 + core)
    twin = (seat, z_hi * 2 + 1 - core)

    barrier = pltpu.get_barrier_semaphore()
    for device in (partner, from_prev0, from_prev1, mirror, twin):
        pl.semaphore_signal(barrier, inc=1, device_id=device, device_id_type=MESH)
    pl.semaphore_wait(barrier, 5)

    def remote(number, source, target, device, arrival=None):
        return pltpu.make_async_remote_copy(
            src_ref=source,
            dst_ref=target,
            send_sem=send_sem.at[number],
            recv_sem=recv_sem.at[number if arrival is None else arrival],
            device_id=device,
            device_id_type=MESH,
        )

    mine = pl.ds(pl.multiple_of(core * half, 8), half)
    own = 2 + side
    mate = 3 - side
    ids = (i_ref, ci), (j_ref, di), (k_ref, fi)

    sent = []
    for n, (source, target) in enumerate(ids):
        sent.append(remote(n, source, target, mirror))
    for n, device in enumerate((to_next0, to_next1)):
        sent.append(remote(4 + n, c_ref.at[mine], cs.at[side, mine], device, 4 + side))
        sent.append(remote(7 + n, d_ref, ds.at[side], device, 7 + side))
        sent.append(remote(10 + n, f_ref, fs.at[side], device, 10 + side))
    sent.append(remote(3, c_ref.at[mine], cs.at[own, mine], partner))
    sent.append(remote(6, d_ref, ds.at[own], partner))
    sent.append(remote(9, f_ref, fs.at[own], partner))
    for copy in sent:
        copy.start()
    cs[own] = c_ref[...]
    ds[own] = d_ref[...]
    fs[own] = f_ref[...]

    counts[...] = jnp.zeros_like(counts)
    count_ids(counts, i_ref, j_ref, k_ref)
    for n, (source, target) in enumerate(ids):
        remote(n, source, target, mirror).wait_recv()
    count_ids(counts, ci, di, fi)
    swap_counts = remote(15, counts, counts_twin, twin)
    swap_counts.start()

    for n, slot in ((3, mate), (4, 0), (5, 1)):
        remote(n, c_ref.at[mine], cs.at[slot, mine], partner).wait_recv()
        forward = remote(9 + n, cs.at[slot, mine], cs.at[slot, mine], twin)
        forward.start()
        sent.append(forward)
    for n, slot in ((6, mate), (7, 0), (8, 1)):
        remote(n, d_ref, ds.at[slot], partner).wait_recv()
        remote(n + 3, f_ref, fs.at[slot], partner).wait_recv()
    swap_counts.wait()
    counts[...] += counts_twin[...]
    theirs = pl.ds(pl.multiple_of((1 - core) * half, 8), half)
    for n, slot in ((12, mate), (13, 0), (14, 1)):
        remote(n, c_ref.at[theirs], cs.at[slot, theirs], twin).wait_recv()

    for p in range(4):
        high, low = split(cs[p])
        lanes = pl.ds(p * width, width)
        ch[:, lanes] = high
        cl[:, lanes] = low
        ct[lanes, :] = cs[p].T
        drow[:, lanes] = ds[p]
        dcol[lanes, :] = jnp.concatenate([ds[p], jnp.zeros((128 - ndose, width), F32)], axis=0).T
    outs = [
        pltpu.make_async_copy(source, target, out_sem.at[n])
        for n, (source, target) in enumerate(((ch, ch_out), (cl, cl_out), (ds, ds_out), (fs, fs_out)))
    ]
    for out in outs:
        out.start()

    doses = ndose // 2
    first_dose = core * doses
    begin = pl.multiple_of(first_dose * nfocus, doses * nfocus)
    n = jnp.concatenate([counts[pl.ds(h * 128 + begin, doses * nfocus), :] for h in range(4)], axis=1)
    fall = jnp.concatenate([fs[p] for p in range(4)], axis=1)
    nh, nl = split(n)
    v = dot(nh, ch[...]) + dot(nh, cl[...]) + dot(nl, ch[...])
    dose_rows = drow[pl.ds(pl.multiple_of(first_dose, doses), doses), :]
    s = jnp.zeros((nfocus, cols), F32)
    per_focus = jnp.zeros((nfocus, nclip), F32)
    for j in range(doses):
        s = s + v[j * nfocus : (j + 1) * nfocus, :] * dose_rows[j : j + 1, :]
        per_focus = per_focus + n[j * nfocus : (j + 1) * nfocus, :]
    s = s + 0.5 * jnp.sum(per_focus, axis=1, keepdims=True) * fall
    gram[...] = full(jnp.concatenate([s, fall], axis=0), jnp.concatenate([fall, s], axis=0), TN)

    lane = lax.broadcasted_iota(jnp.int32, (256, 128), 1)
    swaps = []
    for m in range(2):
        here = pl.ds(m * 256, 256)
        right = pl.ds(m * 256, cols - m * 256)

        def dose(step, _, m=m, here=here, right=right):
            j = first_dose + step
            at = pl.multiple_of(j * nfocus, nfocus)
            nj = jnp.concatenate(
                [jnp.sum(counts[pl.ds(h * 128 + at, nfocus), :], axis=0, keepdims=True) for h in range(4)], axis=1
            )
            dj = jnp.sum(jnp.where(lane == j, dcol[here, :], 0.0), axis=1, keepdims=True)
            row = drow[pl.ds(j, 1), right]
            uh, ul = split(ct[here, :] * nj * dj)
            part = dot(uh, ch[:, right]) + dot(uh, cl[:, right]) + dot(ul, ch[:, right])
            gram[here, right] += part * row
            return 0

        lax.fori_loop(0, doses, dose, 0)
        swap = remote(16 + m, gram.at[here, right], gram_twin.at[here, right], twin)
        swap.start()
        swaps.append(swap)
    for m, swap in enumerate(swaps):
        swap.wait()
        here = pl.ds(m * 256, 256)
        right = pl.ds(m * 256, cols - m * 256)
        gram[here, right] += gram_twin[here, right]
        out = pltpu.make_async_copy(gram.at[here, right], gram_out.at[here, right], out_sem.at[4 + m])
        out.start()
        outs.append(out)
    for copy in sent:
        copy.wait_send()
    for out in outs:
        out.wait()


def call_exchange(seats, clip_cache, dose_scale, focus_term, ids):
    nclip, width = clip_cache.shape
    ndose, nfocus = dose_scale.shape[0], focus_term.shape[0]
    cols = 4 * width
    out = [((nclip, cols), BF16)] * 2 + [((4, ndose, width), F32), ((4, nfocus, width), F32), ((cols, cols), F32)]
    return pl.pallas_call(
        functools.partial(exchange, seats),
        out_shape=[jax.ShapeDtypeStruct(*o) for o in out],
        in_specs=[VMEM] * 6,
        out_specs=[ANY] * 5,
        scratch_shapes=[
            pltpu.VMEM((4, nclip, width), F32),
            pltpu.VMEM((4, ndose, width), F32),
            pltpu.VMEM((4, nfocus, width), F32),
        ]
        + [pltpu.VMEM(ids[0].shape, jnp.int32)] * 3
        + [
            pltpu.VMEM((512, 256), F32),
            pltpu.VMEM((512, 256), F32),
            pltpu.VMEM((nclip, cols), BF16),
            pltpu.VMEM((nclip, cols), BF16),
            pltpu.VMEM((cols, nclip), F32),
            pltpu.VMEM((ndose, cols), F32),
            pltpu.VMEM((cols, 128), F32),
            pltpu.VMEM((cols, cols), F32),
            pltpu.VMEM((cols, cols), F32),
            pltpu.SemaphoreType.DMA((18,)),
            pltpu.SemaphoreType.DMA((18,)),
            pltpu.SemaphoreType.DMA((6,)),
        ],
        compiler_params=pltpu.CompilerParams(
            collective_id=0, has_side_effects=True, vmem_limit_bytes=48 * 2**20
        ),
        name="exchange",
    )(clip_cache, dose_scale, focus_term, *ids)


def compute(
    total, ch_in, cl_in, ds_in, fs_in, gram_in, clips, doses, focuses, out,
    ch, cl, ds, fs, gram, place, where, sem, dcol, table, wd, state, rows, out_sem,
):
    pairs = (gram_in, gram), (fs_in, fs), (ds_in, ds), (ch_in, ch), (cl_in, cl)
    copies = [pltpu.make_async_copy(source, target, sem.at[n]) for n, (source, target) in enumerate(pairs)]
    for copy in copies:
        copy.start()
    nclip, cols = ch.shape
    ndose, nfocus = ds.shape[1], fs.shape[1]
    place[...] = doses[...] * nclip + clips[...]
    copies.append(pltpu.make_async_copy(place, where, sem.at[5]))
    copies[5].start()
    for copy in copies[:3]:
        copy.wait()
    fall = jnp.concatenate([fs[p] for p in range(4)], axis=1)
    for p in range(4):
        dcol[p * 128 : (p + 1) * 128, :] = jnp.concatenate([ds[p], jnp.zeros((128 - ndose, 128), F32)], axis=0).T

    row_i = lax.broadcasted_iota(jnp.int32, (128, 128), 0)
    col_i = lax.broadcasted_iota(jnp.int32, (128, 128), 1)
    squares = jnp.concatenate(
        [
            jnp.sum(jnp.where(row_i == col_i, gram[p * 128 : (p + 1) * 128, p * 128 : (p + 1) * 128], 0.0), axis=0, keepdims=True)
            for p in range(4)
        ],
        axis=1,
    )
    inverse_norm = 1.0 / jnp.sqrt(squares / total + EPSILON)
    norm_col = column(inverse_norm)
    d = squares * inverse_norm * inverse_norm
    d_col = column(d)
    g_prev = gram[:256, :256] * norm_col[:256] * inverse_norm[:, :256]
    g_cross = gram[:256, 256:] * norm_col[:256] * inverse_norm[:, 256:]
    g_own = gram[256:, 256:] * norm_col[256:] * inverse_norm[:, 256:]
    b_prev = 0.5 * g_prev[:128, 128:] / (d_col[:128] + d[:, 128:256])
    b_own = 0.5 * g_own[:128, 128:] / (d_col[256:384] + d[:, 384:])
    (m_prev, m_own), eye = inverses([b_prev, b_own], state)
    z = 2.0 * full(m_prev, b_prev)
    q_right = jnp.concatenate([z, eye - full(b_prev, z, TN)], axis=0)
    q_left = jnp.concatenate([2.0 * m_own - eye, -2.0 * full(b_own, m_own, TN)], axis=0)

    cross = full(full(q_right, g_cross, TN), q_left)
    d_left = jnp.sum(q_right * full(g_prev, q_right), axis=0, keepdims=True)
    d_right = jnp.sum(q_left * full(g_own, q_left), axis=0, keepdims=True)
    b = 0.5 * cross / (column(d_left) + d_right)
    (m,), _ = inverses([b], state)
    z = 2.0 * full(m, b)
    odd = lax.axis_index("panel") % 2 == 1
    top = jnp.where(odd, z, 2.0 * m - eye)
    bottom = jnp.where(odd, eye - full(b, z, TN), -2.0 * full(b, m, TN))
    w = jnp.concatenate([full(q_right, top), full(q_left, bottom)], axis=0) * norm_col
    wd[...] = w

    parts = jnp.concatenate(three(full(fall, w)), axis=0)
    setting = lax.broadcasted_iota(jnp.int32, (3 * nfocus, 128), 0) % nfocus

    def focus(step, _):
        for u in range(8):
            r = step * 8 + u
            chosen = jnp.where(setting == focuses[pl.ds(r, 1), :], 1.0, 0.0).astype(BF16)
            rows[pl.ds(pl.multiple_of(r * 128, 128), 128), :] = dot(chosen, parts, TN)
        return 0

    lax.fori_loop(0, focuses.shape[0] // 8, focus, 0)

    for copy in copies[3:]:
        copy.wait()
    lane = lax.broadcasted_iota(jnp.int32, (cols, 128), 1)

    def rows_of(pair, _):
        scaled = []
        for e in range(2):
            dj = jnp.sum(jnp.where(lane == pair * 2 + e, dcol[...], 0.0), axis=1, keepdims=True)
            scaled.append(wd[...] * dj)
        wh, wl = split(jnp.concatenate(scaled, axis=1))
        for m in range(nclip // 256):
            here = pl.ds(m * 256, 256)
            part = dot(ch[here, :], wh) + dot(cl[here, :], wh) + dot(ch[here, :], wl)
            for e in range(2):
                begin = pl.multiple_of((pair * 2 + e) * nclip + m * 256, 256)
                table[pl.ds(begin, 256), :] = part[:, e * 128 : (e + 1) * 128]
        return 0

    lax.fori_loop(0, ndose // 2, rows_of, 0)

    chunks = out_sem.shape[0]
    height = rows.shape[0] // chunks

    def written(chunk):
        here = pl.ds(pl.multiple_of(chunk * height, height), height)
        return pltpu.make_async_copy(rows.at[here, :], out.at[here, :], out_sem.at[chunk])

    def gather(line, _):
        for u in range(128 // 8):
            begin = pl.multiple_of(line * 128 + u * 8, 8)
            found = jnp.concatenate([table[pl.ds(where[line, u * 8 + e], 1), :] for e in range(8)], axis=0)
            rows[pl.ds(begin, 8), :] = rows[pl.ds(begin, 8), :] + found
        return 0

    for chunk in range(chunks):
        lines = height // 128
        lax.fori_loop(chunk * lines, (chunk + 1) * lines, gather, 0)
        written(chunk).start()
    for chunk in range(chunks):
        written(chunk).wait()


def call_compute(total, ch, cl, ds, fs, gram, ids):
    lines = ids[0].shape[0]
    nclip, cols = ch.shape
    _, ndose, width = ds.shape
    operands = (ch, cl, ds, fs, gram)
    return pl.pallas_call(
        functools.partial(compute, float(total)),
        out_shape=jax.ShapeDtypeStruct((lines * 128, width), F32),
        in_specs=[ANY] * 5 + [VMEM] * 3,
        out_specs=ANY,
        scratch_shapes=[pltpu.VMEM(a.shape, a.dtype) for a in operands]
        + [
            pltpu.VMEM((lines, 128), jnp.int32),
            pltpu.SMEM((lines, 128), jnp.int32),
            pltpu.SemaphoreType.DMA((6,)),
            pltpu.VMEM((cols, 128), F32),
            pltpu.VMEM((ndose * nclip, width), F32),
            pltpu.VMEM((cols, width), F32),
            pltpu.VMEM((2, 2 * width, width), F32),
            pltpu.VMEM((lines * 128, width), F32),
            pltpu.SemaphoreType.DMA((8,)),
        ],
        compiler_params=pltpu.CompilerParams(vmem_limit_bytes=48 * 2**20),
        name="compute",
    )(*operands, *ids)


def shards(clip_cache, dose_scale, focus_term, clip_ids, dose_ids, focus_ids):
    rows = clip_ids.shape[0]
    ids = [a.reshape(rows // 128, 128) for a in (clip_ids, dose_ids, focus_ids)]
    gathered = call_exchange(lax.axis_size("panel"), clip_cache, dose_scale, focus_term, ids)
    return call_compute(rows * lax.axis_size("slab"), *gathered, ids)


def solution(mesh):
    return jax.shard_map(
        shards,
        mesh=mesh,
        in_specs=(
            P(None, "panel"),
            P(None, "panel"),
            P(None, "panel"),
            P("slab"),
            P("slab"),
            P("slab"),
        ),
        out_specs=P("slab", "panel"),
        check_vma=False,
    )
```

time: 123 us -> 80.2 us (0.65)
  Pallas kernels: 114 us -> 75.1 us
  local copies, waits for them, and re-layouts: 8.04 us -> 4.7 us
    pallas_call x2, Pallas kernels: 114 us -> 75.1 us  [the longest x1 48.3 us: call_exchange(): pl.pallas_call(functools.partial(exchange, seats), out_shape=[jax.ShapeDt...]
    unnamed x18 -> x12, local copies, waits for them, and re-layouts: 8.04 us -> 4.7 us
where the time goes in v2:
time: 80.2 us; the launch traced here: 79.8 us
  Pallas kernels  75.1 us (94%)
  local copies, waits for them, and re-layouts  4.7 us (6%)
    pallas_call x1, Pallas kernels, call_exchange(): pl.pallas_call(functools.partial(exchange, seats), out_shape=[jax.ShapeDt...  48.3 us
    pallas_call x1, Pallas kernels, call_compute(): pl.pallas_call(functools.partial(compute, float(total)), out_shape=jax.Sh...  26.8 us
    unnamed x12, local copies, waits for them, and re-layouts  4.7 us

profile of v2, /device:TPU:1, one launch (start us, length us, event | category | flops | bytes accessed | tf_op | source)
XLA Modules:
  0.0 79.8 jit_solution(7064651689022196752)
XLA Ops:
  0.0 0.0 copy-start
  0.0 1.0 %copy-done = f32[1024,128]{1,0:T(8,128)S(1)} copy-done((f32[1024,128]{1,0:T(8,128)S(1)}, f32[1024,128]{1,0:T(8,128)}, u32[]{:S(2)}) %copy-start) | copy-done | bytes 524312
  1.0 0.0 copy-start.1
  1.0 0.8 copy-done.1
  1.8 0.0 copy-start.2
  1.8 0.8 copy-done.2
  2.6 0.0 copy-start.3
  2.6 0.8 copy-done.3
  3.3 0.0 copy-start.4
  3.3 0.7 copy-done.4
  4.0 0.0 copy-start.5
  4.0 0.7 copy-done.5
  4.7 48.3 %exchange.1 = (bf16[1024,512]{1,0:T(8,128)(2,1)S(1)}, bf16[1024,512]{1,0:T(8,128)(2,1)S(1)}, f32[4,16,128]{2,1,0:T(8,128)S(1)}, f32[4,8,128]{2,1,0:T(8,128)S(1)}, f32[512,512]{1,0:T(8,128)S(1)}) custom-call(f32[1024,128]{1,0:T(8,128)S(1)} %copy-done, f32[16,128]{1,0:T(8,128)S(1)} %copy-done.4, f32[8,128]{1,0:T(8,128)S(1)} %copy-done.5, ...), custom_call_target="tpu_custom_call" | custom-call | tf_op jit(solution)/shard_map/exchange/pallas_call | solution.py:261
  53.0 26.8 %compute.1 = f32[8192,128]{1,0:T(8,128)} custom-call(bf16[1024,512]{1,0:T(8,128)(2,1)S(1)} %get-tuple-element.10.ch_in, bf16[1024,512]{1,0:T(8,128)(2,1)S(1)} %get-tuple-element.11.cl_in, f32[4,16,128]{2,1,0:T(8,128)S(1)} %get-tuple-element.12.ds_in, f32[4,8,128]{2,1,0:T(8,128)S(1)} %get-tuple-element.13.fs_in, f32[512,512]{1,0:T(8,128)S(1)} %get-tuple-element.14.gram_in, ...), custom_call_target="tpu_custom_call" | custom-call | tf_op jit(solution)/shard_map/compute/pallas_call | solution.py:406
Async XLA Ops:
  0.0 1.0 %copy-start = (f32[1024,128]{1,0:T(8,128)S(1)}, f32[1024,128]{1,0:T(8,128)}, u32[]{:S(2)}) copy-start(f32[1024,128]{1,0:T(8,128)} %c_ref.1) | copy-start | bytes 1572868
  1.0 0.8 copy-start.1
  1.8 0.8 copy-start.2
  2.6 0.8 copy-start.3
  3.3 0.7 copy-start.4
  4.0 0.7 copy-start.5

commit v3 on v2

--- a/solution.py
+++ b/solution.py
@@ -12,7 +12,6 @@
 F32 = jnp.float32
 BF16 = jnp.bfloat16
 ANY = pl.BlockSpec(memory_space=pl.ANY)
-VMEM = pl.BlockSpec(memory_space=pltpu.VMEM)
 
 
 def split(value):
@@ -98,7 +97,7 @@
 
 def exchange(
     seats, c_ref, d_ref, f_ref, i_ref, j_ref, k_ref, ch_out, cl_out, ds_out, fs_out, gram_out,
-    cs, ds, fs, ci, di, fi, counts, counts_twin, ch, cl, ct, drow, dcol, gram, gram_twin, send_sem, recv_sem, out_sem,
+    cs, ds, fs, ci, di, fi, oi, oj, ok, counts, counts_twin, ch, cl, ct, frow, srow, drow, dcol, gram, gram_twin, send_sem, recv_sem, local_sem, out_sem,
 ):
     seat = lax.axis_index("panel")
     slab = lax.axis_index("slab")
@@ -127,6 +126,11 @@
     mirror = (seat - z_lo + 3 - z_lo, (1 - z_hi) * 2 + core)
     twin = (seat, z_hi * 2 + 1 - core)
 
+    own = 2 + side
+    pairs = (i_ref, oi), (j_ref, oj), (k_ref, ok), (c_ref, cs.at[own]), (d_ref, ds.at[own]), (f_ref, fs.at[own])
+    local = [pltpu.make_async_copy(source, target, local_sem.at[n]) for n, (source, target) in enumerate(pairs)]
+    for copy in local:
+        copy.start()
     barrier = pltpu.get_barrier_semaphore()
     for device in (partner, from_prev0, from_prev1, mirror, twin):
         pl.semaphore_signal(barrier, inc=1, device_id=device, device_id_type=MESH)
@@ -142,104 +146,127 @@
             device_id_type=MESH,
         )
 
-    mine = pl.ds(pl.multiple_of(core * half, 8), half)
-    own = 2 + side
+    mine = pl.ds(pl.multiple_of(core * half, 128), half)
     mate = 3 - side
     ids = (i_ref, ci), (j_ref, di), (k_ref, fi)
 
     sent = []
     for n, (source, target) in enumerate(ids):
         sent.append(remote(n, source, target, mirror))
+    sent.append(remote(3, c_ref.at[mine], cs.at[own, mine], partner))
+    sent.append(remote(6, d_ref, ds.at[own], partner))
+    sent.append(remote(9, f_ref, fs.at[own], partner))
     for n, device in enumerate((to_next0, to_next1)):
         sent.append(remote(4 + n, c_ref.at[mine], cs.at[side, mine], device, 4 + side))
         sent.append(remote(7 + n, d_ref, ds.at[side], device, 7 + side))
         sent.append(remote(10 + n, f_ref, fs.at[side], device, 10 + side))
-    sent.append(remote(3, c_ref.at[mine], cs.at[own, mine], partner))
-    sent.append(remote(6, d_ref, ds.at[own], partner))
-    sent.append(remote(9, f_ref, fs.at[own], partner))
     for copy in sent:
         copy.start()
-    cs[own] = c_ref[...]
-    ds[own] = d_ref[...]
-    fs[own] = f_ref[...]
 
     counts[...] = jnp.zeros_like(counts)
-    count_ids(counts, i_ref, j_ref, k_ref)
+    for copy in local:
+        copy.wait()
+    count_ids(counts, oi, oj, ok)
     for n, (source, target) in enumerate(ids):
         remote(n, source, target, mirror).wait_recv()
     count_ids(counts, ci, di, fi)
-    swap_counts = remote(15, counts, counts_twin, twin)
+    mine_counts = pl.ds(pl.multiple_of(core * 256, 256), 256)
+    theirs_counts = pl.ds(pl.multiple_of((1 - core) * 256, 256), 256)
+    swap_counts = remote(15, counts.at[theirs_counts], counts_twin, twin)
     swap_counts.start()
 
-    for n, slot in ((3, mate), (4, 0), (5, 1)):
+    def arrived(n, slot):
         remote(n, c_ref.at[mine], cs.at[slot, mine], partner).wait_recv()
+        remote(n + 3, d_ref, ds.at[slot], partner).wait_recv()
+        remote(n + 6, f_ref, fs.at[slot], partner).wait_recv()
         forward = remote(9 + n, cs.at[slot, mine], cs.at[slot, mine], twin)
         forward.start()
         sent.append(forward)
-    for n, slot in ((6, mate), (7, 0), (8, 1)):
-        remote(n, d_ref, ds.at[slot], partner).wait_recv()
-        remote(n + 3, f_ref, fs.at[slot], partner).wait_recv()
+
+    def halve(p, rows):
+        high, low = split(cs[p, rows, :])
+        ch[rows, p * width : (p + 1) * width] = high
+        cl[rows, p * width : (p + 1) * width] = low
+
+    def prepare(m):
+        for p in (2 * m, 2 * m + 1):
+            halve(p, mine)
+            lanes = pl.ds(p * width, width)
+            ct[lanes, :] = cs[p, mine, :].T
+            frow[:, lanes] = fs[p]
+            drow[:, lanes] = ds[p]
+            dcol[lanes, :] = jnp.concatenate([ds[p], jnp.zeros((128 - ndose, width), F32)], axis=0).T
+
+    def focus_terms(m):
+        here = pl.ds(m * 256, 256)
+        n = jnp.concatenate([counts[pl.ds(pl.multiple_of(core * 256 + h * 128, 128), 128), :] for h in range(2)], axis=1)
+        nh, nl = split(n)
+        v = dot(nh, ch[mine, here]) + dot(nh, cl[mine, here]) + dot(nl, ch[mine, here])
+        s = jnp.zeros((nfocus, 256), F32)
+        per_focus = jnp.zeros((nfocus, half), F32)
+        for j in range(ndose):
+            s = s + v[j * nfocus : (j + 1) * nfocus, :] * drow[j : j + 1, here]
+            per_focus = per_focus + n[j * nfocus : (j + 1) * nfocus, :]
+        srow[:, here] = s + 0.5 * jnp.sum(per_focus, axis=1, keepdims=True) * frow[:, here]
+        right = pl.ds(m * 256, cols - m * 256)
+        left = jnp.concatenate([srow[:, here], frow[:, here]], axis=0)
+        gram[here, right] = full(left, jnp.concatenate([frow[:, right], srow[:, right]], axis=0), TN)
+
+    lane = lax.broadcasted_iota(jnp.int32, (256, 128), 1)
+    unroll = 4
+
+    def table_terms(m):
+        here = pl.ds(m * 256, 256)
+
+        def dose(step, _):
+            left = []
+            for e in range(unroll):
+                j = step * unroll + e
+                at = pl.multiple_of(core * 256 + j * nfocus, nfocus)
+                nj = jnp.concatenate(
+                    [jnp.sum(counts[pl.ds(at + h * 128, nfocus), :], axis=0, keepdims=True) for h in range(2)], axis=1
+                )
+                dj = jnp.sum(jnp.where(lane == j, dcol[here, :], 0.0), axis=1, keepdims=True)
+                left.append(split(ct[here, :] * nj * dj))
+            for r in range(m, 2):
+                right = pl.ds(r * 256, 256)
+                total = gram[here, right]
+                for e, (uh, ul) in enumerate(left):
+                    part = dot(uh, ch[mine, right]) + dot(uh, cl[mine, right]) + dot(ul, ch[mine, right])
+                    total = total + part * drow[pl.ds(step * unroll + e, 1), right]
+                gram[here, right] = total
+            return 0
+
+        lax.fori_loop(0, ndose // unroll, dose, 0)
+        right = pl.ds(m * 256, cols - m * 256)
+        swap = remote(16 + m, gram.at[here, right], gram_twin.at[here, right], twin)
+        swap.start()
+        return swap
+
+    arrived(3, mate)
+    prepare(1)
     swap_counts.wait()
-    counts[...] += counts_twin[...]
-    theirs = pl.ds(pl.multiple_of((1 - core) * half, 8), half)
+    counts[mine_counts, :] += counts_twin[...]
+    focus_terms(1)
+    swaps = [(1, table_terms(1))]
+    arrived(4, 0)
+    arrived(5, 1)
+    prepare(0)
+    focus_terms(0)
+    swaps.append((0, table_terms(0)))
+
+    theirs = pl.ds(pl.multiple_of((1 - core) * half, 128), half)
     for n, slot in ((12, mate), (13, 0), (14, 1)):
         remote(n, c_ref.at[theirs], cs.at[slot, theirs], twin).wait_recv()
-
     for p in range(4):
-        high, low = split(cs[p])
-        lanes = pl.ds(p * width, width)
-        ch[:, lanes] = high
-        cl[:, lanes] = low
-        ct[lanes, :] = cs[p].T
-        drow[:, lanes] = ds[p]
-        dcol[lanes, :] = jnp.concatenate([ds[p], jnp.zeros((128 - ndose, width), F32)], axis=0).T
+        halve(p, theirs)
     outs = [
         pltpu.make_async_copy(source, target, out_sem.at[n])
         for n, (source, target) in enumerate(((ch, ch_out), (cl, cl_out), (ds, ds_out), (fs, fs_out)))
     ]
     for out in outs:
         out.start()
-
-    doses = ndose // 2
-    first_dose = core * doses
-    begin = pl.multiple_of(first_dose * nfocus, doses * nfocus)
-    n = jnp.concatenate([counts[pl.ds(h * 128 + begin, doses * nfocus), :] for h in range(4)], axis=1)
-    fall = jnp.concatenate([fs[p] for p in range(4)], axis=1)
-    nh, nl = split(n)
-    v = dot(nh, ch[...]) + dot(nh, cl[...]) + dot(nl, ch[...])
-    dose_rows = drow[pl.ds(pl.multiple_of(first_dose, doses), doses), :]
-    s = jnp.zeros((nfocus, cols), F32)
-    per_focus = jnp.zeros((nfocus, nclip), F32)
-    for j in range(doses):
-        s = s + v[j * nfocus : (j + 1) * nfocus, :] * dose_rows[j : j + 1, :]
-        per_focus = per_focus + n[j * nfocus : (j + 1) * nfocus, :]
-    s = s + 0.5 * jnp.sum(per_focus, axis=1, keepdims=True) * fall
-    gram[...] = full(jnp.concatenate([s, fall], axis=0), jnp.concatenate([fall, s], axis=0), TN)
-
-    lane = lax.broadcasted_iota(jnp.int32, (256, 128), 1)
-    swaps = []
-    for m in range(2):
-        here = pl.ds(m * 256, 256)
-        right = pl.ds(m * 256, cols - m * 256)
-
-        def dose(step, _, m=m, here=here, right=right):
-            j = first_dose + step
-            at = pl.multiple_of(j * nfocus, nfocus)
-            nj = jnp.concatenate(
-                [jnp.sum(counts[pl.ds(h * 128 + at, nfocus), :], axis=0, keepdims=True) for h in range(4)], axis=1
-            )
-            dj = jnp.sum(jnp.where(lane == j, dcol[here, :], 0.0), axis=1, keepdims=True)
-            row = drow[pl.ds(j, 1), right]
-            uh, ul = split(ct[here, :] * nj * dj)
-            part = dot(uh, ch[:, right]) + dot(uh, cl[:, right]) + dot(ul, ch[:, right])
-            gram[here, right] += part * row
-            return 0
-
-        lax.fori_loop(0, doses, dose, 0)
-        swap = remote(16 + m, gram.at[here, right], gram_twin.at[here, right], twin)
-        swap.start()
-        swaps.append(swap)
-    for m, swap in enumerate(swaps):
+    for m, swap in swaps:
         swap.wait()
         here = pl.ds(m * 256, 256)
         right = pl.ds(m * 256, cols - m * 256)
@@ -261,20 +288,22 @@
     return pl.pallas_call(
         functools.partial(exchange, seats),
         out_shape=[jax.ShapeDtypeStruct(*o) for o in out],
-        in_specs=[VMEM] * 6,
+        in_specs=[ANY] * 6,
         out_specs=[ANY] * 5,
         scratch_shapes=[
             pltpu.VMEM((4, nclip, width), F32),
             pltpu.VMEM((4, ndose, width), F32),
             pltpu.VMEM((4, nfocus, width), F32),
         ]
-        + [pltpu.VMEM(ids[0].shape, jnp.int32)] * 3
+        + [pltpu.VMEM(ids[0].shape, jnp.int32)] * 6
         + [
             pltpu.VMEM((512, 256), F32),
-            pltpu.VMEM((512, 256), F32),
+            pltpu.VMEM((256, 256), F32),
             pltpu.VMEM((nclip, cols), BF16),
             pltpu.VMEM((nclip, cols), BF16),
-            pltpu.VMEM((cols, nclip), F32),
+            pltpu.VMEM((cols, nclip // 2), F32),
+            pltpu.VMEM((nfocus, cols), F32),
+            pltpu.VMEM((nfocus, cols), F32),
             pltpu.VMEM((ndose, cols), F32),
             pltpu.VMEM((cols, 128), F32),
             pltpu.VMEM((cols, cols), F32),
@@ -282,28 +311,32 @@
             pltpu.SemaphoreType.DMA((18,)),
             pltpu.SemaphoreType.DMA((18,)),
             pltpu.SemaphoreType.DMA((6,)),
+            pltpu.SemaphoreType.DMA((6,)),
         ],
         compiler_params=pltpu.CompilerParams(
-            collective_id=0, has_side_effects=True, vmem_limit_bytes=48 * 2**20
+            collective_id=0, has_side_effects=True, vmem_limit_bytes=56 * 2**20
         ),
         name="exchange",
     )(clip_cache, dose_scale, focus_term, *ids)
 
 
 def compute(
-    total, ch_in, cl_in, ds_in, fs_in, gram_in, clips, doses, focuses, out,
-    ch, cl, ds, fs, gram, place, where, sem, dcol, table, wd, state, rows, out_sem,
+    total, ch_in, cl_in, ds_in, fs_in, gram_in, clips_in, doses_in, focuses_in, out,
+    ch, cl, ds, fs, gram, clips, doses, focuses, place, where, sem, dcol, table, wd, state, rows, out_sem,
 ):
-    pairs = (gram_in, gram), (fs_in, fs), (ds_in, ds), (ch_in, ch), (cl_in, cl)
+    pairs = (clips_in, clips), (doses_in, doses), (focuses_in, focuses), (gram_in, gram), (fs_in, fs), (ds_in, ds)
+    pairs += (ch_in, ch), (cl_in, cl)
     copies = [pltpu.make_async_copy(source, target, sem.at[n]) for n, (source, target) in enumerate(pairs)]
     for copy in copies:
         copy.start()
     nclip, cols = ch.shape
     ndose, nfocus = ds.shape[1], fs.shape[1]
+    for copy in copies[:3]:
+        copy.wait()
     place[...] = doses[...] * nclip + clips[...]
-    copies.append(pltpu.make_async_copy(place, where, sem.at[5]))
-    copies[5].start()
-    for copy in copies[:3]:
+    copies.append(pltpu.make_async_copy(place, where, sem.at[8]))
+    copies[8].start()
+    for copy in copies[3:6]:
         copy.wait()
     fall = jnp.concatenate([fs[p] for p in range(4)], axis=1)
     for p in range(4):
@@ -356,7 +389,7 @@
 
     lax.fori_loop(0, focuses.shape[0] // 8, focus, 0)
 
-    for copy in copies[3:]:
+    for copy in copies[6:]:
         copy.wait()
     lane = lax.broadcasted_iota(jnp.int32, (cols, 128), 1)
 
@@ -374,7 +407,7 @@
                 table[pl.ds(begin, 256), :] = part[:, e * 128 : (e + 1) * 128]
         return 0
 
-    lax.fori_loop(0, ndose // 2, rows_of, 0)
+    lax.fori_loop(0, ndose // 4, lambda q, c: rows_of(q * 2 + 1, rows_of(q * 2, c)), 0)
 
     chunks = out_sem.shape[0]
     height = rows.shape[0] // chunks
@@ -402,17 +435,17 @@
     lines = ids[0].shape[0]
     nclip, cols = ch.shape
     _, ndose, width = ds.shape
-    operands = (ch, cl, ds, fs, gram)
+    operands = (ch, cl, ds, fs, gram, *ids)
     return pl.pallas_call(
         functools.partial(compute, float(total)),
         out_shape=jax.ShapeDtypeStruct((lines * 128, width), F32),
-        in_specs=[ANY] * 5 + [VMEM] * 3,
+        in_specs=[ANY] * 8,
         out_specs=ANY,
         scratch_shapes=[pltpu.VMEM(a.shape, a.dtype) for a in operands]
         + [
             pltpu.VMEM((lines, 128), jnp.int32),
             pltpu.SMEM((lines, 128), jnp.int32),
-            pltpu.SemaphoreType.DMA((6,)),
+            pltpu.SemaphoreType.DMA((9,)),
             pltpu.VMEM((cols, 128), F32),
             pltpu.VMEM((ndose * nclip, width), F32),
             pltpu.VMEM((cols, width), F32),
@@ -420,9 +453,9 @@
             pltpu.VMEM((lines * 128, width), F32),
             pltpu.SemaphoreType.DMA((8,)),
         ],
-        compiler_params=pltpu.CompilerParams(vmem_limit_bytes=48 * 2**20),
+        compiler_params=pltpu.CompilerParams(vmem_limit_bytes=56 * 2**20),
         name="compute",
-    )(*operands, *ids)
+    )(*operands)
 
 
 def shards(clip_cache, dose_scale, focus_term, clip_ids, dose_ids, focus_ids):

time: 80.2 us -> 67.7 us (0.84)
  Pallas kernels: 75.1 us -> 67.6 us
  local copies, waits for them, and re-layouts: 4.7 us -> 0 us
    pallas_call x1, Pallas kernels: 48.3 us -> 41 us  [call_exchange(): pl.pallas_call(functools.partial(exchange, seats), out_shape=[jax.ShapeDt...]
    unnamed x12 -> x0, local copies, waits for them, and re-layouts: 4.7 us -> none
where the time goes in v3:
time: 67.7 us
  Pallas kernels  67.6 us (100%)
    pallas_call x1, Pallas kernels, call_exchange(): pl.pallas_call(functools.partial(exchange, seats), out_shape=[jax.ShapeDt...  41 us
    pallas_call x1, Pallas kernels, call_compute(): pl.pallas_call(functools.partial(compute, float(total)), out_shape=jax.Sh...  26.7 us

profile of v3, /device:TPU:1, one launch (start us, length us, event | category | flops | bytes accessed | tf_op | source)
XLA Modules:
  0.0 67.7 jit_solution(16012982643307987979)
XLA Ops:
  0.0 41.0 %exchange.1 = (bf16[1024,512]{1,0:T(8,128)(2,1)}, bf16[1024,512]{1,0:T(8,128)(2,1)}, f32[4,16,128]{2,1,0:T(8,128)}, f32[4,8,128]{2,1,0:T(8,128)}, f32[512,512]{1,0:T(8,128)}) custom-call(f32[1024,128]{1,0:T(8,128)} %c_ref.1, f32[16,128]{1,0:T(8,128)} %d_ref.1, f32[8,128]{1,0:T(8,128)} %f_ref.1, s32[64,128]{1,0:T(8,128)} %bitcast.3, s32[64,128]{1,0:T(8,128)} %bitcast.5, ...), custom_call_target="tpu_custom_call" | custom-call | tf_op jit(solution)/shard_map/exchange/pallas_call | solution.py:288
  41.0 26.7 %compute.1 = f32[8192,128]{1,0:T(8,128)} custom-call(bf16[1024,512]{1,0:T(8,128)(2,1)} %get-tuple-element.10.ch_in, bf16[1024,512]{1,0:T(8,128)(2,1)} %get-tuple-element.11.cl_in, f32[4,16,128]{2,1,0:T(8,128)} %get-tuple-element.12.ds_in, f32[4,8,128]{2,1,0:T(8,128)} %get-tuple-element.13.fs_in, f32[512,512]{1,0:T(8,128)} %get-tuple-element.14.gram_in, ...), custom_call_target="tpu_custom_call" | custom-call | tf_op jit(solution)/shard_map/compute/pallas_call | solution.py:439

commit v4 on v3

--- a/solution.py
+++ b/solution.py
@@ -35,6 +35,12 @@
     b1, b2, b3 = three(b)
     small = dot(a2, b2, dims) + dot(a1, b3, dims) + dot(a3, b1, dims)
     return dot(a1, b1, dims) + (dot(a1, b2, dims) + dot(a2, b1, dims) + small)
+
+
+def good(a, b, dims=((1,), (0,))):
+    a1, a2 = split(a)
+    b1, b2 = split(b)
+    return dot(a1, b1, dims) + (dot(a1, b2, dims) + dot(a2, b1, dims))
 
 
 TN = ((0,), (0,))
@@ -322,8 +328,10 @@
 
 def compute(
     total, ch_in, cl_in, ds_in, fs_in, gram_in, clips_in, doses_in, focuses_in, out,
-    ch, cl, ds, fs, gram, clips, doses, focuses, place, where, sem, dcol, table, wd, state, rows, out_sem,
+    ch, cl, ds, fs, gram, clips, doses, focuses, place, where0, where1, where2, where3, sem, where_sem,
+    dcol, table, wd, state, rows, out_sem,
 ):
+    where = (where0, where1, where2, where3)
     pairs = (clips_in, clips), (doses_in, doses), (focuses_in, focuses), (gram_in, gram), (fs_in, fs), (ds_in, ds)
     pairs += (ch_in, ch), (cl_in, cl)
     copies = [pltpu.make_async_copy(source, target, sem.at[n]) for n, (source, target) in enumerate(pairs)]
@@ -334,8 +342,8 @@
     for copy in copies[:3]:
         copy.wait()
     place[...] = doses[...] * nclip + clips[...]
-    copies.append(pltpu.make_async_copy(place, where, sem.at[8]))
-    copies[8].start()
+    for e in range(len(where)):
+        pltpu.make_async_copy(place.at[pl.ds(e * where[e].shape[0], where[e].shape[0]), :], where[e], where_sem.at[e]).start()
     for copy in copies[3:6]:
         copy.wait()
     fall = jnp.concatenate([fs[p] for p in range(4)], axis=1)
@@ -361,20 +369,20 @@
     b_prev = 0.5 * g_prev[:128, 128:] / (d_col[:128] + d[:, 128:256])
     b_own = 0.5 * g_own[:128, 128:] / (d_col[256:384] + d[:, 384:])
     (m_prev, m_own), eye = inverses([b_prev, b_own], state)
-    z = 2.0 * full(m_prev, b_prev)
-    q_right = jnp.concatenate([z, eye - full(b_prev, z, TN)], axis=0)
-    q_left = jnp.concatenate([2.0 * m_own - eye, -2.0 * full(b_own, m_own, TN)], axis=0)
-
-    cross = full(full(q_right, g_cross, TN), q_left)
-    d_left = jnp.sum(q_right * full(g_prev, q_right), axis=0, keepdims=True)
-    d_right = jnp.sum(q_left * full(g_own, q_left), axis=0, keepdims=True)
+    z = 2.0 * good(m_prev, b_prev)
+    q_right = jnp.concatenate([z, eye - good(b_prev, z, TN)], axis=0)
+    q_left = jnp.concatenate([2.0 * m_own - eye, -2.0 * good(b_own, m_own, TN)], axis=0)
+
+    cross = good(good(q_right, g_cross, TN), q_left)
+    d_left = jnp.sum(q_right * good(g_prev, q_right), axis=0, keepdims=True)
+    d_right = jnp.sum(q_left * good(g_own, q_left), axis=0, keepdims=True)
     b = 0.5 * cross / (column(d_left) + d_right)
     (m,), _ = inverses([b], state)
-    z = 2.0 * full(m, b)
+    z = 2.0 * good(m, b)
     odd = lax.axis_index("panel") % 2 == 1
     top = jnp.where(odd, z, 2.0 * m - eye)
-    bottom = jnp.where(odd, eye - full(b, z, TN), -2.0 * full(b, m, TN))
-    w = jnp.concatenate([full(q_right, top), full(q_left, bottom)], axis=0) * norm_col
+    bottom = jnp.where(odd, eye - good(b, z, TN), -2.0 * good(b, m, TN))
+    w = jnp.concatenate([good(q_right, top), good(q_left, bottom)], axis=0) * norm_col
     wd[...] = w
 
     parts = jnp.concatenate(three(full(fall, w)), axis=0)
@@ -409,26 +417,44 @@
 
     lax.fori_loop(0, ndose // 4, lambda q, c: rows_of(q * 2 + 1, rows_of(q * 2, c)), 0)
 
-    chunks = out_sem.shape[0]
-    height = rows.shape[0] // chunks
-
-    def written(chunk):
-        here = pl.ds(pl.multiple_of(chunk * height, height), height)
-        return pltpu.make_async_copy(rows.at[here, :], out.at[here, :], out_sem.at[chunk])
-
-    def gather(line, _):
-        for u in range(128 // 8):
-            begin = pl.multiple_of(line * 128 + u * 8, 8)
-            found = jnp.concatenate([table[pl.ds(where[line, u * 8 + e], 1), :] for e in range(8)], axis=0)
-            rows[pl.ds(begin, 8), :] = rows[pl.ds(begin, 8), :] + found
+    windows = len(where)
+    lines = where[0].shape[0]
+    steps = place.shape[0] // (windows * lines)
+    height = lines * 128
+
+    def window(step, e):
+        begin = pl.multiple_of((step * windows + e) * lines, lines)
+        return pltpu.make_async_copy(place.at[pl.ds(begin, lines), :], where[e], where_sem.at[e])
+
+    def written(step, e):
+        here = pl.ds(pl.multiple_of((step * windows + e) * height, height), height)
+        return pltpu.make_async_copy(rows.at[here, :], out.at[here, :], out_sem.at[e])
+
+    def gather(step, _):
+        for e in range(windows):
+            window(step, e).wait()
+            begin = pl.multiple_of((step * windows + e) * height, height)
+            for u in range(height // 8):
+                found = jnp.concatenate(
+                    [table[pl.ds(where[e][u // 16, u % 16 * 8 + r], 1), :] for r in range(8)], axis=0
+                )
+                here = pl.ds(begin + u * 8, 8)
+                rows[here, :] = rows[here, :] + found
+
+            @pl.when(step + 1 < steps)
+            def _(e=e):
+                window(step + 1, e).start()
+
+            @pl.when(step > 0)
+            def _(e=e):
+                written(step - 1, e).wait()
+
+            written(step, e).start()
         return 0
 
-    for chunk in range(chunks):
-        lines = height // 128
-        lax.fori_loop(chunk * lines, (chunk + 1) * lines, gather, 0)
-        written(chunk).start()
-    for chunk in range(chunks):
-        written(chunk).wait()
+    lax.fori_loop(0, steps, gather, 0)
+    for e in range(windows):
+        written(steps - 1, e).wait()
 
 
 def call_compute(total, ch, cl, ds, fs, gram, ids):
@@ -444,14 +470,17 @@
         scratch_shapes=[pltpu.VMEM(a.shape, a.dtype) for a in operands]
         + [
             pltpu.VMEM((lines, 128), jnp.int32),
-            pltpu.SMEM((lines, 128), jnp.int32),
-            pltpu.SemaphoreType.DMA((9,)),
+        ]
+        + [pltpu.SMEM((4, 128), jnp.int32)] * 4
+        + [
+            pltpu.SemaphoreType.DMA((8,)),
+            pltpu.SemaphoreType.DMA((4,)),
             pltpu.VMEM((cols, 128), F32),
             pltpu.VMEM((ndose * nclip, width), F32),
             pltpu.VMEM((cols, width), F32),
             pltpu.VMEM((2, 2 * width, width), F32),
             pltpu.VMEM((lines * 128, width), F32),
-            pltpu.SemaphoreType.DMA((8,)),
+            pltpu.SemaphoreType.DMA((4,)),
         ],
         compiler_params=pltpu.CompilerParams(vmem_limit_bytes=56 * 2**20),
         name="compute",

time: 67.7 us -> 64.5 us (0.953)
  Pallas kernels: 67.6 us -> 64.4 us
    pallas_call x1, Pallas kernels: 26.7 us -> 23.4 us  [call_compute(): pl.pallas_call(functools.partial(compute, float(total)), out_shape=jax.Sh...]
where the time goes in v4:
time: 64.5 us; the launch traced here: 64.4 us
  Pallas kernels  64.4 us (100%)
    pallas_call x1, Pallas kernels, call_exchange(): pl.pallas_call(functools.partial(exchange, seats), out_shape=[jax.ShapeDt...  41 us
    pallas_call x1, Pallas kernels, call_compute(): pl.pallas_call(functools.partial(compute, float(total)), out_shape=jax.Sh...  23.4 us

profile of v4, /device:TPU:1, one launch (start us, length us, event | category | flops | bytes accessed | tf_op | source)
XLA Modules:
  0.0 64.4 jit_solution(5084293741753004644)
XLA Ops:
  0.0 41.0 %exchange.1 = (bf16[1024,512]{1,0:T(8,128)(2,1)}, bf16[1024,512]{1,0:T(8,128)(2,1)}, f32[4,16,128]{2,1,0:T(8,128)}, f32[4,8,128]{2,1,0:T(8,128)}, f32[512,512]{1,0:T(8,128)}) custom-call(f32[1024,128]{1,0:T(8,128)} %c_ref.1, f32[16,128]{1,0:T(8,128)} %d_ref.1, f32[8,128]{1,0:T(8,128)} %f_ref.1, s32[64,128]{1,0:T(8,128)} %bitcast.3, s32[64,128]{1,0:T(8,128)} %bitcast.5, ...), custom_call_target="tpu_custom_call" | custom-call | tf_op jit(solution)/shard_map/exchange/pallas_call | solution.py:294
  41.0 23.4 %compute.1 = f32[8192,128]{1,0:T(8,128)} custom-call(bf16[1024,512]{1,0:T(8,128)(2,1)} %get-tuple-element.10.ch_in, bf16[1024,512]{1,0:T(8,128)(2,1)} %get-tuple-element.11.cl_in, f32[4,16,128]{2,1,0:T(8,128)} %get-tuple-element.12.ds_in, f32[4,8,128]{2,1,0:T(8,128)} %get-tuple-element.13.fs_in, f32[512,512]{1,0:T(8,128)} %get-tuple-element.14.gram_in, ...), custom_call_target="tpu_custom_call" | custom-call | tf_op jit(solution)/shard_map/compute/pallas_call | solution.py:465

commit v5 on v4

--- a/solution.py
+++ b/solution.py
@@ -205,6 +205,7 @@
 
     def focus_terms(m):
         here = pl.ds(m * 256, 256)
+        right = pl.ds(256, 256)
         n = jnp.concatenate([counts[pl.ds(pl.multiple_of(core * 256 + h * 128, 128), 128), :] for h in range(2)], axis=1)
         nh, nl = split(n)
         v = dot(nh, ch[mine, here]) + dot(nh, cl[mine, here]) + dot(nl, ch[mine, here])
@@ -214,11 +215,11 @@
             s = s + v[j * nfocus : (j + 1) * nfocus, :] * drow[j : j + 1, here]
             per_focus = per_focus + n[j * nfocus : (j + 1) * nfocus, :]
         srow[:, here] = s + 0.5 * jnp.sum(per_focus, axis=1, keepdims=True) * frow[:, here]
-        right = pl.ds(m * 256, cols - m * 256)
         left = jnp.concatenate([srow[:, here], frow[:, here]], axis=0)
         gram[here, right] = full(left, jnp.concatenate([frow[:, right], srow[:, right]], axis=0), TN)
 
     lane = lax.broadcasted_iota(jnp.int32, (256, 128), 1)
+    right = pl.ds(256, 256)
     unroll = 4
 
     def table_terms(m):
@@ -234,17 +235,14 @@
                 )
                 dj = jnp.sum(jnp.where(lane == j, dcol[here, :], 0.0), axis=1, keepdims=True)
                 left.append(split(ct[here, :] * nj * dj))
-            for r in range(m, 2):
-                right = pl.ds(r * 256, 256)
-                total = gram[here, right]
-                for e, (uh, ul) in enumerate(left):
-                    part = dot(uh, ch[mine, right]) + dot(uh, cl[mine, right]) + dot(ul, ch[mine, right])
-                    total = total + part * drow[pl.ds(step * unroll + e, 1), right]
-                gram[here, right] = total
+            total = gram[here, right]
+            for e, (uh, ul) in enumerate(left):
+                part = dot(uh, ch[mine, right]) + dot(uh, cl[mine, right]) + dot(ul, ch[mine, right])
+                total = total + part * drow[pl.ds(step * unroll + e, 1), right]
+            gram[here, right] = total
             return 0
 
         lax.fori_loop(0, ndose // unroll, dose, 0)
-        right = pl.ds(m * 256, cols - m * 256)
         swap = remote(16 + m, gram.at[here, right], gram_twin.at[here, right], twin)
         swap.start()
         return swap
@@ -254,32 +252,46 @@
     swap_counts.wait()
     counts[mine_counts, :] += counts_twin[...]
     focus_terms(1)
-    swaps = [(1, table_terms(1))]
+    swap_own = table_terms(1)
     arrived(4, 0)
     arrived(5, 1)
     prepare(0)
     focus_terms(0)
-    swaps.append((0, table_terms(0)))
-
+    swap_own.wait()
+    gram[right, right] += gram_twin[right, right]
+    target = (base + 3 - side) % seats
+    sent.append(
+        remote(
+            18,
+            gram.at[pl.ds(pl.multiple_of(256 + core * 128, 128), 128), right],
+            gram.at[pl.ds(pl.multiple_of(core * 128, 128), 128), pl.ds(0, 256)],
+            (target, near(target) * 2 + core),
+        )
+    )
+    sent[-1].start()
+    swap_cross = table_terms(0)
+
+    here = pl.ds(0, 256)
+    half_rows = gram.at[pl.ds(pl.multiple_of(core * 128, 128), 128), here]
+    remote(18, half_rows, half_rows, twin).wait_recv()
+    sent.append(remote(19, half_rows, half_rows, twin))
+    sent[-1].start()
     theirs = pl.ds(pl.multiple_of((1 - core) * half, 128), half)
     for n, slot in ((12, mate), (13, 0), (14, 1)):
         remote(n, c_ref.at[theirs], cs.at[slot, theirs], twin).wait_recv()
     for p in range(4):
         halve(p, theirs)
-    outs = [
-        pltpu.make_async_copy(source, target, out_sem.at[n])
-        for n, (source, target) in enumerate(((ch, ch_out), (cl, cl_out), (ds, ds_out), (fs, fs_out)))
-    ]
+    places = ((ch, ch_out), (cl, cl_out), (ds, ds_out), (fs, fs_out))
+    outs = [pltpu.make_async_copy(source, target, out_sem.at[n]) for n, (source, target) in enumerate(places)]
+    outs.append(pltpu.make_async_copy(gram.at[right, right], gram_out.at[right, right], out_sem.at[4]))
     for out in outs:
         out.start()
-    for m, swap in swaps:
-        swap.wait()
-        here = pl.ds(m * 256, 256)
-        right = pl.ds(m * 256, cols - m * 256)
-        gram[here, right] += gram_twin[here, right]
-        out = pltpu.make_async_copy(gram.at[here, right], gram_out.at[here, right], out_sem.at[4 + m])
-        out.start()
-        outs.append(out)
+    swap_cross.wait()
+    gram[here, right] += gram_twin[here, right]
+    other_rows = gram.at[pl.ds(pl.multiple_of((1 - core) * 128, 128), 128), here]
+    remote(19, other_rows, other_rows, twin).wait_recv()
+    outs.append(pltpu.make_async_copy(gram.at[here, :], gram_out.at[here, :], out_sem.at[5]))
+    outs[-1].start()
     for copy in sent:
         copy.wait_send()
     for out in outs:
@@ -314,8 +326,8 @@
             pltpu.VMEM((cols, 128), F32),
             pltpu.VMEM((cols, cols), F32),
             pltpu.VMEM((cols, cols), F32),
-            pltpu.SemaphoreType.DMA((18,)),
-            pltpu.SemaphoreType.DMA((18,)),
+            pltpu.SemaphoreType.DMA((20,)),
+            pltpu.SemaphoreType.DMA((20,)),
             pltpu.SemaphoreType.DMA((6,)),
             pltpu.SemaphoreType.DMA((6,)),
         ],

time: 64.5 us -> 62.3 us (0.966)
  Pallas kernels: 64.4 us -> 62.2 us
    pallas_call x1, Pallas kernels: 41 us -> 38.8 us  [call_exchange(): pl.pallas_call(functools.partial(exchange, seats), out_shape=[jax.ShapeDt...]
where the time goes in v5:
time: 62.3 us; the launch traced here: 62.2 us
  Pallas kernels  62.2 us (100%)
    pallas_call x1, Pallas kernels, call_exchange(): pl.pallas_call(functools.partial(exchange, seats), out_shape=[jax.ShapeDt...  38.8 us
    pallas_call x1, Pallas kernels, call_compute(): pl.pallas_call(functools.partial(compute, float(total)), out_shape=jax.Sh...  23.4 us

profile of v5, /device:TPU:1, one launch (start us, length us, event | category | flops | bytes accessed | tf_op | source)
XLA Modules:
  0.0 62.2 jit_solution(13998812262612534779)
XLA Ops:
  0.0 38.8 %exchange.1 = (bf16[1024,512]{1,0:T(8,128)(2,1)}, bf16[1024,512]{1,0:T(8,128)(2,1)}, f32[4,16,128]{2,1,0:T(8,128)}, f32[4,8,128]{2,1,0:T(8,128)}, f32[512,512]{1,0:T(8,128)}) custom-call(f32[1024,128]{1,0:T(8,128)} %c_ref.1, f32[16,128]{1,0:T(8,128)} %d_ref.1, f32[8,128]{1,0:T(8,128)} %f_ref.1, s32[64,128]{1,0:T(8,128)} %bitcast.3, s32[64,128]{1,0:T(8,128)} %bitcast.5, ...), custom_call_target="tpu_custom_call" | custom-call | tf_op jit(solution)/shard_map/exchange/pallas_call | solution.py:306
  38.8 23.4 %compute.1 = f32[8192,128]{1,0:T(8,128)} custom-call(bf16[1024,512]{1,0:T(8,128)(2,1)} %get-tuple-element.10.ch_in, bf16[1024,512]{1,0:T(8,128)(2,1)} %get-tuple-element.11.cl_in, f32[4,16,128]{2,1,0:T(8,128)} %get-tuple-element.12.ds_in, f32[4,8,128]{2,1,0:T(8,128)} %get-tuple-element.13.fs_in, f32[512,512]{1,0:T(8,128)} %get-tuple-element.14.gram_in, ...), custom_call_target="tpu_custom_call" | custom-call | tf_op jit(solution)/shard_map/compute/pallas_call | solution.py:477

commit v6 on v5

--- a/solution.py
+++ b/solution.py
@@ -85,7 +85,7 @@
 def count_ids(counts, clips, doses, focuses):
     rows = 8
 
-    def count(step, _):
+    def part(step):
         here = pl.ds(pl.multiple_of(step * rows, rows), rows)
         clip = clips[here, :]
         first = (clip // 256) * 128 + doses[here, :] * 8 + focuses[here, :]
@@ -95,10 +95,13 @@
             row = first[r : r + 1, :]
             tall.append(jnp.concatenate(onehot(row, 256, 0.0) + onehot(row, 256, 256.0), axis=0))
             wide.append(jnp.concatenate(onehot(second[r : r + 1, :], 256, 0.0), axis=0))
-        counts[...] += dot(jnp.concatenate(tall, axis=1), jnp.concatenate(wide, axis=1), NT)
+        return dot(jnp.concatenate(tall, axis=1), jnp.concatenate(wide, axis=1), NT)
+
+    def count(step, _):
+        counts[...] += part(step * 2) + part(step * 2 + 1)
         return 0
 
-    lax.fori_loop(0, clips.shape[0] // rows, count, 0)
+    lax.fori_loop(0, clips.shape[0] // rows // 2, count, 0)
 
 
 def exchange(
@@ -220,25 +223,30 @@
 
     lane = lax.broadcasted_iota(jnp.int32, (256, 128), 1)
     right = pl.ds(256, 256)
-    unroll = 4
+    unroll, stack = 8, 4
 
     def table_terms(m):
         here = pl.ds(m * 256, 256)
 
         def dose(step, _):
-            left = []
-            for e in range(unroll):
-                j = step * unroll + e
-                at = pl.multiple_of(core * 256 + j * nfocus, nfocus)
-                nj = jnp.concatenate(
-                    [jnp.sum(counts[pl.ds(at + h * 128, nfocus), :], axis=0, keepdims=True) for h in range(2)], axis=1
-                )
-                dj = jnp.sum(jnp.where(lane == j, dcol[here, :], 0.0), axis=1, keepdims=True)
-                left.append(split(ct[here, :] * nj * dj))
             total = gram[here, right]
-            for e, (uh, ul) in enumerate(left):
-                part = dot(uh, ch[mine, right]) + dot(uh, cl[mine, right]) + dot(ul, ch[mine, right])
-                total = total + part * drow[pl.ds(step * unroll + e, 1), right]
+            for first in range(0, unroll, stack):
+                left, outer = [], []
+                for e in range(first, first + stack):
+                    j = step * unroll + e
+                    at = pl.multiple_of(core * 256 + j * nfocus, nfocus)
+                    nj = jnp.concatenate(
+                        [jnp.sum(counts[pl.ds(at + h * 128, nfocus), :], axis=0, keepdims=True) for h in range(2)],
+                        axis=1,
+                    )
+                    left.append(split(ct[here, :] * nj))
+                    dj = jnp.sum(jnp.where(lane == j, dcol[here, :], 0.0), axis=1, keepdims=True)
+                    outer.append(dj * drow[pl.ds(j, 1), right])
+                uh = jnp.concatenate([high for high, _ in left], axis=0)
+                ul = jnp.concatenate([low for _, low in left], axis=0)
+                part = dot(uh, ch[mine, right]) + dot(ul, ch[mine, right]) + dot(uh, cl[mine, right])
+                for e in range(stack):
+                    total = total + part[e * 256 : (e + 1) * 256, :] * outer[e]
             gram[here, right] = total
             return 0
 
@@ -400,18 +408,11 @@
     parts = jnp.concatenate(three(full(fall, w)), axis=0)
     setting = lax.broadcasted_iota(jnp.int32, (3 * nfocus, 128), 0) % nfocus
 
-    def focus(step, _):
-        for u in range(8):
-            r = step * 8 + u
-            chosen = jnp.where(setting == focuses[pl.ds(r, 1), :], 1.0, 0.0).astype(BF16)
-            rows[pl.ds(pl.multiple_of(r * 128, 128), 128), :] = dot(chosen, parts, TN)
-        return 0
-
-    lax.fori_loop(0, focuses.shape[0] // 8, focus, 0)
-
     for copy in copies[6:]:
         copy.wait()
     lane = lax.broadcasted_iota(jnp.int32, (cols, 128), 1)
+
+    height = 512
 
     def rows_of(pair, _):
         scaled = []
@@ -419,12 +420,12 @@
             dj = jnp.sum(jnp.where(lane == pair * 2 + e, dcol[...], 0.0), axis=1, keepdims=True)
             scaled.append(wd[...] * dj)
         wh, wl = split(jnp.concatenate(scaled, axis=1))
-        for m in range(nclip // 256):
-            here = pl.ds(m * 256, 256)
+        for m in range(nclip // height):
+            here = pl.ds(m * height, height)
             part = dot(ch[here, :], wh) + dot(cl[here, :], wh) + dot(ch[here, :], wl)
             for e in range(2):
-                begin = pl.multiple_of((pair * 2 + e) * nclip + m * 256, 256)
-                table[pl.ds(begin, 256), :] = part[:, e * 128 : (e + 1) * 128]
+                begin = pl.multiple_of((pair * 2 + e) * nclip + m * height, height)
+                table[pl.ds(begin, height), :] = part[:, e * 128 : (e + 1) * 128]
         return 0
 
     lax.fori_loop(0, ndose // 4, lambda q, c: rows_of(q * 2 + 1, rows_of(q * 2, c)), 0)
@@ -446,12 +447,12 @@
         for e in range(windows):
             window(step, e).wait()
             begin = pl.multiple_of((step * windows + e) * height, height)
-            for u in range(height // 8):
-                found = jnp.concatenate(
-                    [table[pl.ds(where[e][u // 16, u % 16 * 8 + r], 1), :] for r in range(8)], axis=0
-                )
-                here = pl.ds(begin + u * 8, 8)
-                rows[here, :] = rows[here, :] + found
+            for line in range(lines):
+                ids = focuses[pl.ds((step * windows + e) * lines + line, 1), :]
+                part = dot(jnp.where(setting == ids, 1.0, 0.0).astype(BF16), parts, TN)
+                for u in range(0, 128, 8):
+                    found = jnp.concatenate([table[pl.ds(where[e][line, u + r], 1), :] for r in range(8)], axis=0)
+                    rows[pl.ds(begin + line * 128 + u, 8), :] = part[u : u + 8, :] + found
 
             @pl.when(step + 1 < steps)
             def _(e=e):

time: 62.3 us -> 61.1 us (0.981)
  Pallas kernels: 62.2 us -> 61 us
    pallas_call x1, Pallas kernels: 38.8 us -> 37.9 us  [call_exchange(): pl.pallas_call(functools.partial(exchange, seats), out_shape=[jax.ShapeDt...]
where the time goes in v6:
time: 61.1 us; the launch traced here: 61 us
  Pallas kernels  61 us (100%)
    pallas_call x1, Pallas kernels, call_exchange(): pl.pallas_call(functools.partial(exchange, seats), out_shape=[jax.ShapeDt...  37.9 us
    pallas_call x1, Pallas kernels, call_compute(): pl.pallas_call(functools.partial(compute, float(total)), out_shape=jax.Sh...  23.2 us

profile of v6, /device:TPU:1, one launch (start us, length us, event | category | flops | bytes accessed | tf_op | source)
XLA Modules:
  0.0 61.0 jit_solution(8392149673715259093)
XLA Ops:
  0.0 37.9 %exchange.1 = (bf16[1024,512]{1,0:T(8,128)(2,1)}, bf16[1024,512]{1,0:T(8,128)(2,1)}, f32[4,16,128]{2,1,0:T(8,128)}, f32[4,8,128]{2,1,0:T(8,128)}, f32[512,512]{1,0:T(8,128)}) custom-call(f32[1024,128]{1,0:T(8,128)} %c_ref.1, f32[16,128]{1,0:T(8,128)} %d_ref.1, f32[8,128]{1,0:T(8,128)} %f_ref.1, s32[64,128]{1,0:T(8,128)} %bitcast.3, s32[64,128]{1,0:T(8,128)} %bitcast.5, ...), custom_call_target="tpu_custom_call" | custom-call | tf_op jit(solution)/shard_map/exchange/pallas_call | solution.py:314
  37.9 23.2 %compute.1 = f32[8192,128]{1,0:T(8,128)} custom-call(bf16[1024,512]{1,0:T(8,128)(2,1)} %get-tuple-element.10.ch_in, bf16[1024,512]{1,0:T(8,128)(2,1)} %get-tuple-element.11.cl_in, f32[4,16,128]{2,1,0:T(8,128)} %get-tuple-element.12.ds_in, f32[4,8,128]{2,1,0:T(8,128)} %get-tuple-element.13.fs_in, f32[512,512]{1,0:T(8,128)} %get-tuple-element.14.gram_in, ...), custom_call_target="tpu_custom_call" | custom-call | tf_op jit(solution)/shard_map/compute/pallas_call | solution.py:478

commit v7 on v6

--- a/solution.py
+++ b/solution.py
@@ -165,10 +165,13 @@
     sent.append(remote(3, c_ref.at[mine], cs.at[own, mine], partner))
     sent.append(remote(6, d_ref, ds.at[own], partner))
     sent.append(remote(9, f_ref, fs.at[own], partner))
+    quarter = [pl.ds(pl.multiple_of(core * half + e * half // 2, 128), half // 2) for e in range(2)]
     for n, device in enumerate((to_next0, to_next1)):
-        sent.append(remote(4 + n, c_ref.at[mine], cs.at[side, mine], device, 4 + side))
+        sent.append(remote(4 + n, c_ref.at[quarter[0]], cs.at[side, quarter[0]], device, 4 + side))
         sent.append(remote(7 + n, d_ref, ds.at[side], device, 7 + side))
         sent.append(remote(10 + n, f_ref, fs.at[side], device, 10 + side))
+    for n, device in enumerate((to_next0, to_next1)):
+        sent.append(remote(20 + n, c_ref.at[quarter[1]], cs.at[side, quarter[1]], device, 20 + side))
     for copy in sent:
         copy.start()
 
@@ -184,11 +187,15 @@
     swap_counts = remote(15, counts.at[theirs_counts], counts_twin, twin)
     swap_counts.start()
 
-    def arrived(n, slot):
-        remote(n, c_ref.at[mine], cs.at[slot, mine], partner).wait_recv()
+    def settings(n, slot):
         remote(n + 3, d_ref, ds.at[slot], partner).wait_recv()
         remote(n + 6, f_ref, fs.at[slot], partner).wait_recv()
-        forward = remote(9 + n, cs.at[slot, mine], cs.at[slot, mine], twin)
+
+    def arrived(n, slot, rows):
+        remote(n, c_ref.at[rows], cs.at[slot, rows], partner).wait_recv()
+
+    def pass_on(n, slot):
+        forward = remote(n, cs.at[slot, mine], cs.at[slot, mine], twin)
         forward.start()
         sent.append(forward)
 
@@ -197,11 +204,14 @@
         ch[rows, p * width : (p + 1) * width] = high
         cl[rows, p * width : (p + 1) * width] = low
 
-    def prepare(m):
+    def prepare(m, rows, clips):
         for p in (2 * m, 2 * m + 1):
-            halve(p, mine)
+            halve(p, rows)
+            ct[p * width : (p + 1) * width, clips] = cs[p, rows, :].T
+
+    def prepare_settings(m):
+        for p in (2 * m, 2 * m + 1):
             lanes = pl.ds(p * width, width)
-            ct[lanes, :] = cs[p, mine, :].T
             frow[:, lanes] = fs[p]
             drow[:, lanes] = ds[p]
             dcol[lanes, :] = jnp.concatenate([ds[p], jnp.zeros((128 - ndose, width), F32)], axis=0).T
@@ -219,14 +229,15 @@
             per_focus = per_focus + n[j * nfocus : (j + 1) * nfocus, :]
         srow[:, here] = s + 0.5 * jnp.sum(per_focus, axis=1, keepdims=True) * frow[:, here]
         left = jnp.concatenate([srow[:, here], frow[:, here]], axis=0)
-        gram[here, right] = full(left, jnp.concatenate([frow[:, right], srow[:, right]], axis=0), TN)
+        gram[here, right] += full(left, jnp.concatenate([frow[:, right], srow[:, right]], axis=0), TN)
 
     lane = lax.broadcasted_iota(jnp.int32, (256, 128), 1)
     right = pl.ds(256, 256)
     unroll, stack = 8, 4
 
-    def table_terms(m):
+    def table_terms(m, rows, parts):
         here = pl.ds(m * 256, 256)
+        clips = pl.ds(parts[0] * 256, len(parts) * 256)
 
         def dose(step, _):
             total = gram[here, right]
@@ -236,35 +247,44 @@
                     j = step * unroll + e
                     at = pl.multiple_of(core * 256 + j * nfocus, nfocus)
                     nj = jnp.concatenate(
-                        [jnp.sum(counts[pl.ds(at + h * 128, nfocus), :], axis=0, keepdims=True) for h in range(2)],
+                        [jnp.sum(counts[pl.ds(at + h * 128, nfocus), :], axis=0, keepdims=True) for h in parts],
                         axis=1,
                     )
-                    left.append(split(ct[here, :] * nj))
+                    left.append(split(ct[here, clips] * nj))
                     dj = jnp.sum(jnp.where(lane == j, dcol[here, :], 0.0), axis=1, keepdims=True)
                     outer.append(dj * drow[pl.ds(j, 1), right])
                 uh = jnp.concatenate([high for high, _ in left], axis=0)
                 ul = jnp.concatenate([low for _, low in left], axis=0)
-                part = dot(uh, ch[mine, right]) + dot(ul, ch[mine, right]) + dot(uh, cl[mine, right])
+                part = dot(uh, ch[rows, right]) + dot(ul, ch[rows, right]) + dot(uh, cl[rows, right])
                 for e in range(stack):
                     total = total + part[e * 256 : (e + 1) * 256, :] * outer[e]
             gram[here, right] = total
             return 0
 
         lax.fori_loop(0, ndose // unroll, dose, 0)
+
+    def swap_terms(m):
+        here = pl.ds(m * 256, 256)
         swap = remote(16 + m, gram.at[here, right], gram_twin.at[here, right], twin)
         swap.start()
         return swap
 
-    arrived(3, mate)
-    prepare(1)
+    gram[:, right] = jnp.zeros((cols, 256), F32)
+    arrived(3, mate, mine)
+    settings(3, mate)
+    pass_on(12, mate)
+    prepare(1, mine, pl.ds(0, half))
+    prepare_settings(1)
     swap_counts.wait()
     counts[mine_counts, :] += counts_twin[...]
     focus_terms(1)
-    swap_own = table_terms(1)
-    arrived(4, 0)
-    arrived(5, 1)
-    prepare(0)
-    focus_terms(0)
+    table_terms(1, mine, (0, 1))
+    swap_own = swap_terms(1)
+    for slot in range(2):
+        arrived(4 + slot, slot, quarter[0])
+        settings(4 + slot, slot)
+    prepare_settings(0)
+    prepare(0, quarter[0], pl.ds(0, half // 2))
     swap_own.wait()
     gram[right, right] += gram_twin[right, right]
     target = (base + 3 - side) % seats
@@ -277,7 +297,14 @@
         )
     )
     sent[-1].start()
-    swap_cross = table_terms(0)
+    table_terms(0, quarter[0], (0,))
+    for slot in range(2):
+        arrived(20 + slot, slot, quarter[1])
+        pass_on(13 + slot, slot)
+    prepare(0, quarter[1], pl.ds(half // 2, half // 2))
+    focus_terms(0)
+    table_terms(0, quarter[1], (1,))
+    swap_cross = swap_terms(0)
 
     here = pl.ds(0, 256)
     half_rows = gram.at[pl.ds(pl.multiple_of(core * 128, 128), 128), here]
@@ -334,8 +361,8 @@
             pltpu.VMEM((cols, 128), F32),
             pltpu.VMEM((cols, cols), F32),
             pltpu.VMEM((cols, cols), F32),
-            pltpu.SemaphoreType.DMA((20,)),
-            pltpu.SemaphoreType.DMA((20,)),
+            pltpu.SemaphoreType.DMA((22,)),
+            pltpu.SemaphoreType.DMA((22,)),
             pltpu.SemaphoreType.DMA((6,)),
             pltpu.SemaphoreType.DMA((6,)),
         ],

time: 61.1 us -> 60.5 us (level)
  Pallas kernels: 61 us -> 60.2 us
where the time goes in v7:
time: 60.5 us; the launch traced here: 60.3 us
  Pallas kernels  60.2 us (100%)
    pallas_call x1, Pallas kernels, call_exchange(): pl.pallas_call(functools.partial(exchange, seats), out_shape=[jax.ShapeDt...  37.4 us
    pallas_call x1, Pallas kernels, call_compute(): pl.pallas_call(functools.partial(compute, float(total)), out_shape=jax.Sh...  22.9 us

profile of v7, /device:TPU:1, one launch (start us, length us, event | category | flops | bytes accessed | tf_op | source)
XLA Modules:
  0.0 60.3 jit_solution(4522276908723153537)
XLA Ops:
  0.0 37.4 %exchange.1 = (bf16[1024,512]{1,0:T(8,128)(2,1)}, bf16[1024,512]{1,0:T(8,128)(2,1)}, f32[4,16,128]{2,1,0:T(8,128)}, f32[4,8,128]{2,1,0:T(8,128)}, f32[512,512]{1,0:T(8,128)}) custom-call(f32[1024,128]{1,0:T(8,128)} %c_ref.1, f32[16,128]{1,0:T(8,128)} %d_ref.1, f32[8,128]{1,0:T(8,128)} %f_ref.1, s32[64,128]{1,0:T(8,128)} %bitcast.3, s32[64,128]{1,0:T(8,128)} %bitcast.5, ...), custom_call_target="tpu_custom_call" | custom-call | tf_op jit(solution)/shard_map/exchange/pallas_call | solution.py:341
  37.4 22.9 %compute.1 = f32[8192,128]{1,0:T(8,128)} custom-call(bf16[1024,512]{1,0:T(8,128)(2,1)} %get-tuple-element.10.ch_in, bf16[1024,512]{1,0:T(8,128)(2,1)} %get-tuple-element.11.cl_in, f32[4,16,128]{2,1,0:T(8,128)} %get-tuple-element.12.ds_in, f32[4,8,128]{2,1,0:T(8,128)} %get-tuple-element.13.fs_in, f32[512,512]{1,0:T(8,128)} %get-tuple-element.14.gram_in, ...), custom_call_target="tpu_custom_call" | custom-call | tf_op jit(solution)/shard_map/compute/pallas_call | solution.py:505
